TPU v7x, 512 devices: a whole 4x8x8 slice. The times are simulated.
512 devices in a mesh: seq: 32 (over x, y), head: 16 (over z, core).
Axes of the slice: x: 4, y: 8, z: 8, core: 2. Of those that a mesh axis runs over, the one named last changes fastest.
Arguments:
- tokens: bfloat16 [8192, 2048], P('seq'), may hold values from -18 to 18
- qkv_weight: bfloat16 [3, 2048, 2048], P(None, None, 'head'), may hold values from -1 to 1
- beta_logit: float32 [16, 8192], P('head', 'seq'), may hold values from -5.8 to -3.5
- log_decay: float32 [16, 8192], P('head', 'seq'), may hold values from -1 to 0
- out_grad: bfloat16 [8192, 2048], P('seq', 'head'), may hold values from -24 to 24
Outputs:
- input_grad: bfloat16 [8192, 2048], P('seq', 'head')
All inputs are finite; a program needn't handle non-finite values.
Results may differ from a plain program's by a relative error of at most 0.008.
Values may be sent and summed in bfloat16 or wider, within the bound.
A program may use at most 64 MiB of HBM per device.

v0:
```python
import jax
import jax.numpy as jnp
from jax import lax
from jax.sharding import PartitionSpec as P

HIGH = lax.Precision.HIGHEST


def prefix(part, axis, combine, identity, reverse):
    count = lax.axis_size(axis)
    place = lax.axis_index(axis)
    ahead = count - 1 - place if reverse else place
    gathered = lax.all_gather(part, axis)
    state = jnp.zeros_like(part) + jnp.asarray(identity, part.dtype)

    def one(turn, state):
        source = count - 1 - turn if reverse else turn
        return combine(state, lax.dynamic_index_in_dim(gathered, source, 0, False))

    return lax.fori_loop(0, ahead, one, state)


def product(left, right):
    return jnp.dot(left, right, precision=HIGH)


def unit_rows(tensor):
    return tensor * lax.rsqrt(jnp.sum(tensor * tensor, axis=-1, keepdims=True) + 1e-06)


def block_step(memory, pieces, want_out):
    queries, key_rows, values, gate_rows, strengths = pieces
    block_size = key_rows.shape[0]
    row_ids = lax.broadcasted_iota(jnp.int32, (block_size, block_size), 0)
    col_ids = lax.broadcasted_iota(jnp.int32, (block_size, block_size), 1)
    causal = row_ids >= col_ids
    strict = row_ids > col_ids
    cumulative = jnp.cumsum(gate_rows)
    spread = jnp.where(causal, cumulative[:, None] - cumulative[None, :], 0.0)
    decays = jnp.where(causal, jnp.exp(spread), 0.0)
    opening = jnp.exp(cumulative)[:, None]
    couplings = jnp.where(strict, strengths[:, None] * decays * product(key_rows, key_rows.T), 0.0)
    system = jnp.eye(block_size, dtype=jnp.float32) + couplings
    target = strengths[:, None] * (values - opening * product(key_rows, memory))
    update = jax.scipy.linalg.solve_triangular(system, target, lower=True, unit_diagonal=True)
    fading = jnp.exp(cumulative[-1] - cumulative)[:, None]
    new_memory = jnp.exp(cumulative[-1]) * memory + product((key_rows * fading).T, update)
    if want_out:
        result = opening * product(queries, memory) + product(
            decays * product(queries, key_rows.T), update
        )
        return (new_memory, result)
    return (new_memory, None)


def run_segment(queries, key_rows, values, gate_rows, strengths, memory, want_out):
    length = key_rows.shape[0]
    block_size = min(64, length)
    blocks = length // block_size

    def blocked(tensor):
        return tensor.reshape((blocks, block_size) + tensor.shape[1:])

    def advance(carried, pieces):
        return block_step(carried, pieces, want_out)

    closing, results = lax.scan(
        advance,
        memory,
        (
            blocked(queries),
            blocked(key_rows),
            blocked(values),
            blocked(gate_rows),
            blocked(strengths),
        ),
    )
    if want_out:
        results = results.reshape(length, results.shape[-1])
    return (closing, results)


def transit(key_rows, values, gate_rows, strengths):
    head_width = key_rows.shape[-1]
    unit_keys = unit_rows(key_rows)
    opening = jnp.concatenate(
        [jnp.eye(head_width, dtype=jnp.float32), jnp.zeros((head_width, head_width), jnp.float32)],
        axis=1,
    )
    widened = jnp.concatenate([jnp.zeros_like(values), values], axis=1)
    closing, _ = run_segment(unit_keys, unit_keys, widened, gate_rows, strengths, opening, False)
    return closing


def seed_grad(queries, key_rows, gate_rows, strengths, cotangent):
    head_width = key_rows.shape[-1]
    unit_queries = unit_rows(queries)
    unit_keys = unit_rows(key_rows)
    vacant = jnp.zeros_like(unit_keys)

    def outputs(memory):
        return run_segment(unit_queries, unit_keys, vacant, gate_rows, strengths, memory, True)[1]

    _, pullback = jax.vjp(outputs, jnp.zeros((head_width, head_width), jnp.float32))
    return pullback(cotangent)[0]


def pull_back(queries, key_rows, values, gate_rows, strengths, memory, cotangent, beyond):

    def forward(query_in, key_in, value_in):
        return run_segment(
            unit_rows(query_in), unit_rows(key_in), value_in, gate_rows, strengths, memory, True
        )

    _, pullback = jax.vjp(forward, queries, key_rows, values)
    return pullback((beyond, cotangent))


def compose(earlier, later):
    head_width = earlier.shape[-2]
    leading = later[..., :head_width]
    shifted = jnp.einsum("hij,hjk->hik", leading, earlier, precision=HIGH)
    return shifted + jnp.concatenate([jnp.zeros_like(leading), later[..., head_width:]], axis=-1)


def split_product(grads, weights):
    upper = grads.astype(jnp.bfloat16)
    lower = (grads - upper.astype(jnp.float32)).astype(jnp.bfloat16)
    first = jnp.einsum("ptc,pdc->td", upper, weights, preferred_element_type=jnp.float32)
    second = jnp.einsum("ptc,pdc->td", lower, weights, preferred_element_type=jnp.float32)
    return first + second


def on_device(tokens, qkv_weight, beta_logit, log_decay, out_grad):
    heads_here, length = beta_logit.shape
    head_width = qkv_weight.shape[-1] // heads_here

    def per_head(tensor):
        return tensor.reshape(length, heads_here, head_width).transpose(1, 0, 2)

    projected = [
        per_head(jnp.dot(tokens, qkv_weight[member], preferred_element_type=jnp.float32))
        for member in range(3)
    ]
    queries, key_rows, values = projected
    strengths = jax.nn.sigmoid(beta_logit)
    cotangent = per_head(out_grad.astype(jnp.float32))
    transitions = jax.vmap(transit)(key_rows, values, log_decay, strengths)
    seeds = jax.vmap(seed_grad)(queries, key_rows, log_decay, strengths, cotangent)
    eyes = jnp.broadcast_to(
        jnp.eye(head_width, dtype=jnp.float32), (heads_here, head_width, head_width)
    )
    identity = jnp.concatenate(
        [eyes, jnp.zeros((heads_here, head_width, head_width), jnp.float32)], axis=-1
    )
    reached = prefix(transitions, "seq", compose, identity, False)
    entering = reached[..., head_width:]
    mirrored = jnp.concatenate([jnp.swapaxes(transitions[..., :head_width], 1, 2), seeds], axis=-1)
    returned = prefix(mirrored, "seq", compose, identity, True)
    leaving = returned[..., head_width:]
    grads = jax.vmap(pull_back)(
        queries, key_rows, values, log_decay, strengths, entering, cotangent, leaving
    )
    stacked = jnp.stack(grads)
    qkv_grad = stacked.transpose(0, 2, 1, 3).reshape(3, length, heads_here * head_width)
    partial_sums = split_product(qkv_grad, qkv_weight)
    assembled = lax.psum_scatter(partial_sums, "head", scatter_dimension=1, tiled=True)
    return assembled.astype(jnp.bfloat16)


def solution(mesh):
    return jax.shard_map(
        on_device,
        mesh=mesh,
        in_specs=(
            P("seq", None),
            P(None, None, "head"),
            P("head", "seq"),
            P("head", "seq"),
            P("seq", "head"),
        ),
        out_specs=P("seq", "head"),
        check_vma=False,
    )
```

profile of v0, /device:TPU:1, one launch (start us, length us, event | category | flops | bytes accessed | tf_op | source)
XLA Modules:
  0.0 495.6 jit_solution(18396469995858636878)
XLA Ops:
  12.3 11.8 %while.137 = (s32[]{:T(128)}, f32[4,1,64,1]{2,3,1,0:T(1,128)S(1)}, f32[4,1,64,1]{2,3,1,0:T(1,128)S(1)}, f32[4,1,64,64]{3,2,1,0:T(8,128)S(1)}, f32[4,1]{1,0:T(4,1...) while((s32[]{:T(128)}, f32[4,1,64,1]{2,3,1,0:T(1,128)S(1)}, ...), condition=%wide.region_7.8_spmd.clone.clone, body=%wide.region_5.7_spmd.clone.clone.sunk | while | flops 12660738 | bytes 370361 | solution.py:67
  24.1 29.8 %while.139 = (s32[]{:T(128)}, f32[1,128,128]{1,2,0:T(8,128)S(1)}, f32[4,1,64,1]{2,3,1,0:T(1,128)S(1)}, f32[4,1,64,128]{3,2,1,0:T(8,128)S(1)}, f32[4,1,64,128]{3,...) while((s32[]{:T(128)}, f32[1,128,128]{1,2,0:T(8,128)S(1)}, ...), condition=%wide.region_9.11_spmd.clone, body=%wide.region_8.10_spmd.clone.sunk | while | flops 50475076 | bytes 808123 | solution.py:67
  24.8 4.9 custom-call.43
  32.2 4.9 custom-call.43
  39.7 4.9 custom-call.43
  47.1 4.9 custom-call.43
  54.1 33.0 %while.133 = (s32[]{:T(128)}, f32[1,128,256]{2,1,0:T(8,128)S(1)}, f32[4,1,64]{2,1,0:T(1,128)S(1)}, f32[4,1,64,128]{3,2,1,0:T(8,128)S(1)}, f32[4,1,64]{2,1,0:T(1,...) while((s32[]{:T(128)}, f32[1,128,256]{2,1,0:T(8,128)S(1)}, f32[4,1,64]{2,1,0:T(1,128)S(1)}, ...), condition=%wide.region_3.4_spmd, body=%wide.region_1.3_spmd.sunk | while | flops 69398592 | bytes 859265 | solution.py:67
  56.0 4.9 custom-call.39
  64.3 4.9 custom-call.39
  72.5 4.9 custom-call.39
  80.8 4.9 custom-call.39
  88.8 89.1 %all-gather.5.cloned.1.call-done = f32[32,128,256]{2,1,0:T(8,128)} async-done(((f32[1,128,256]{2,1,0:T(8,128)}), f32[32,128,256]{2,1,0:T(8,128)}) %all-gather.5.cloned.1.call-update) | async-done | bytes 4194320 | tf_op jit(solution)/shard_map/all_gather | solution.py:13
  177.9 38.7 %while.134 = (s32[]{:T(128)}, f32[1,128,256]{2,1,0:T(8,128)S(1)}, s32[]{:T(128)}, f32[32,1,128,256]{3,2,1,0:T(8,128)}, s32[]{:T(128)}, /*index=5*/s32[]{:T(128)}, s32[]{:T(128)}, s32[]{:T(128)}) while((s32[]{:T(128)}, f32[1,128,256]{2,1,0:T(8,128)S(1)}, s32[]{:T(128)}, f32[32,1,128,256]{3,2,1,0:T(8,128)}, s32[]{:T(128)}, ...), condition=%wide.region_11.13_spmd, body=%wide.region_10.12_spmd.sunk | while | flops 50364420 | bytes 1048711 | solution.py:20
  216.7 49.0 %all-gather.7.cloned.1.call-done = f32[32,128,256]{2,1,0:T(8,128)} async-done(((f32[1,128,256]{2,1,0:T(8,128)}), f32[32,128,256]{2,1,0:T(8,128)}) %all-gather.7.cloned.1.call-update) | async-done | bytes 4194320 | tf_op jit(solution)/shard_map/all_gather | solution.py:13
  267.8 44.6 %while.138 = (s32[]{:T(128)}, f32[1,128,128]{2,1,0:T(8,128)S(1)}, f32[4,1,128,64]{3,2,1,0:T(8,128)S(1)}, f32[4,1,64,64]{3,2,1,0:T(8,128)}, f32[4,1,128,128]{3,2,...) while((s32[]{:T(128)}, f32[1,128,128]{2,1,0:T(8,128)S(1)}, ...), condition=%wide.region_16.18_spmd.clone.clone, body=%wide.region_14.17_spmd.clone.clone.sunk | while | flops 44224640 | bytes 1261069 | solution.py:67
  270.7 4.9 custom-call.42
  281.9 4.9 custom-call.42
  293.0 4.9 custom-call.42
  304.2 4.9 custom-call.42
  313.1 71.8 %while.136 = (s32[]{:T(128)}, f32[1,128,128]{1,2,0:T(8,128)S(1)}, f32[4,1,64,128]{3,2,1,0:T(8,128)S(1)}, f32[4,1,64,128]{3,2,1,0:T(8,128)S(1)}, f32[4,1,64,128]{...) while((s32[]{:T(128)}, f32[1,128,128]{1,2,0:T(8,128)S(1)}, ...), condition=%wide.region_18.20_spmd.clone, body=%wide.region_17.19_spmd.clone.sunk | while | flops 129208384 | bytes 2158369 | solution.py:67
  321.5 4.9 custom-call.41
  357.4 4.9 custom-call.41
  368.3 4.9 custom-call.40
  389.8 97.8 %reduce-scatter.2.cloned.1.call-done = f32[256,128]{1,0:T(8,128)} async-done(((f32[256,2048]{1,0:T(8,128)}), f32[256,128]{1,0:T(8,128)}) %reduce-scatter.2.cloned.1.call-update) | async-done | bytes 131088 | tf_op jit(solution)/shard_map/reduce_scatter | solution.py:167
  (491 shorter events, 161.0 us)
Async XLA Ops:
  6.5 1.2 copy-start
  6.5 2.8 copy-start.3
  6.5 171.4 %all-gather.5.cloned.1.call-start = ((), (), s32[]{:S(2)}) async-start(), calls=%async_computation.2 | async-start | bytes 4325376 | tf_op jit(solution)/shard_map/all_gather | solution.py:13
  9.3 1.0 copy-start.6
  9.8 2.4 copy-start.8
  9.8 1.3 copy-start.12
  9.8 2.1 copy-start.13
  12.2 11.9 %copy-start.5 = (bf16[256,128]{1,0:T(8,128)(2,1)S(1)}, bf16[256,128]{1,0:T(8,128)(2,1)}, u32[]{:S(2)}) copy-start(bf16[256,128]{1,0:T(8,128)(2,1)} %param.25) | copy-start | bytes 196612
  87.1 0.9 copy-start.1
  87.1 1.7 copy-start.11
  87.9 177.8 %all-gather.7.cloned.1.call-start = ((), (), s32[]{:S(2)}) async-start(), calls=%async_computation.3 | async-start | bytes 4325376 | tf_op jit(solution)/shard_map/all_gather | solution.py:13
  88.7 398.9 %reduce-scatter.2.cloned.1.call-start = ((), (), s32[]{:S(2)}) async-start(), calls=%async_computation.1 | async-start | bytes 2228224 | tf_op jit(solution)/shard_map/reduce_scatter | solution.py:167
  216.7 49.0 %copy-start.2 = (f32[1,128,256]{1,2,0:T(8,128)}, f32[1,128,256]{1,2,0:T(8,128)S(1)}, u32[]{:S(2)}) copy-start(f32[1,128,256]{1,2,0:T(8,128)S(1)} %copy.31) | copy-start | bytes 393220
  267.8 45.2 %slice-start = ((f32[1,128,256]{1,2,0:T(8,128)}), f32[1,128,128]{1,2,0:T(8,128)S(1)}, s32[]{:S(2)}) async-start(f32[1,128,256]{1,2,0:T(8,128)} %copy-done.2), calls=%async_computation.4 | async-start | bytes 131072 | tf_op jit(solution)/shard_map/slice | solution.py:160
  312.5 0.6 copy-start.10
  313.1 71.9 %copy-start.9 = (f32[256]{0:T(256)S(1)}, f32[256]{0:T(256)}, u32[]{:S(2)}) copy-start(f32[256]{0:T(256)} %copy-done.8) | copy-start | bytes 3076
  313.1 72.1 %copy-start.7 = (f32[256]{0:T(256)S(1)}, f32[256]{0:T(256)}, u32[]{:S(2)}) copy-start(f32[256]{0:T(256)} %copy-done.6) | copy-start | bytes 3076
  385.4 2.3 copy-start.4
Sparse Core Ops, SparseCore 0:
  88.0 89.8 all-gather.4
  181.1 84.5 all-gather.6
  389.9 97.6 reduce-scatter.1
where the time goes:
time: 500 us; the launch traced here: 496 us
  waiting for transfers between devices  237 us (47%)
  other arithmetic  119 us (24%)
  matrix products  62.3 us (12%)
  local copies, waits for them, and re-layouts  51.9 us (10%)
  between operations  13.6 us (3%)
  loops' own time  11.7 us (2%)
    all_gather x2, waiting for transfers between devices, prefix(): gathered = lax.all_gather(part, axis)  138 us
    another operation x52, other arithmetic, block_step(): jax.scipy.linalg.solve_triangular(system, target, lower=True, unit_diagon...  99.3 us
    reduce_scatter x1, waiting for transfers between devices, on_device(): lax.psum_scatter(partial_sums, 'head', scatter_dimension=1, tiled=True)  97.8 us
    dot_general x100, matrix products, product(): return jnp.dot(left, right, precision=HIGH)  39.4 us
    squeeze x31, local copies, waits for them, and re-layouts, one(): return combine(state, lax.dynamic_index_in_dim(gathered, source, 0, False))  28.5 us
    another operation x5, loops' own time, run_segment(): lax.scan(advance, memory, (blocked(queries), blocked(key_rows), blocked(v...  10.1 us
  transfers between devices with their start and end apart: 3, of which 3 were waited for; matrix products, arithmetic and copies ran while one was open for 8% of the time, Pallas kernels for 0%

commit v1 on v0

v1 whole, which is shorter than its diff:
```python
import functools

import jax
import jax.numpy as jnp
from jax import lax
from jax.experimental import pallas as pl
from jax.experimental.pallas import tpu as pltpu
from jax.sharding import PartitionSpec as P

F32 = jnp.float32
BF16 = jnp.bfloat16
MESH = pl.DeviceIdType.MESH
X, Y, Z = 4, 8, 8
C, DK = 256, 128
B_AT, R_AT, A_AT, Z_AT, ROWS = 0, 128, 256, 272, 400
PIECES = ((R_AT, 144), (B_AT, 128), (Z_AT, 128))


def dot(a, b, ca=1, cb=0):
    return lax.dot_general(
        a.astype(BF16), b.astype(BF16), (((ca,), (cb,)), ((), ())), preferred_element_type=F32
    )


def split(a):
    upper = a.astype(BF16)
    return upper, (a - upper.astype(F32)).astype(BF16)


def thirds(a):
    upper, rest = split(a)
    middle = rest
    lower = (a - upper.astype(F32) - middle.astype(F32)).astype(BF16)
    return upper, middle, lower


def unit_inverse_less_identity(low, rows, cols):
    def same(shift):
        return (rows >> shift) == (cols >> shift)

    power = jnp.where(same(5), low, 0.0)
    off = -power
    for _ in range(4):
        power = dot(power, power)
        off = off + power + dot(off, power)
    for shift in (5, 6, 7):
        inside = jnp.where(same(shift + 1) & ~same(shift), low, 0.0)
        left = inside + dot(off, inside)
        off = off - left - dot(left, off)
    return off


def kernel(
    tok, wgt, bl, ld, og, out,
    ag, xg, pre, core_out, core_in, own, up_out, dn_out, up_in, dn_in, fin,
    up_s, up_r, dn_s, dn_r, x_s, x_r, c_s, c_r, zu_s, zu_r, zd_s, zd_r,
):
    seq, head = lax.axis_index("seq"), lax.axis_index("head")
    x, y = seq // Y, seq % Y
    z, core = head // 2, head % 2

    def at(dx=0, dy=0, dz=0, dc=0):
        return (
            ((x + dx) % X) * Y + (y + dy + Y) % Y,
            ((z + dz + Z) % Z) * 2 + (core + dc) % 2,
        )

    peers = [at(dy=1), at(dy=-1), at(dx=1), at(dx=2), at(dx=3), at(dc=1), at(dz=1), at(dz=-1)]
    barrier = pltpu.get_barrier_semaphore()
    for peer in peers:
        pl.semaphore_signal(barrier, inc=1, device_id=peer, device_id_type=MESH)

    proj = [
        lax.dot_general(tok[...], wgt[p], (((1,), (0,)), ((), ())), preferred_element_type=F32)
        for p in range(3)
    ]
    q_inv = lax.rsqrt(jnp.sum(proj[0] * proj[0], axis=1, keepdims=True) + 1e-6)
    k_inv = lax.rsqrt(jnp.sum(proj[1] * proj[1], axis=1, keepdims=True) + 1e-6)
    qn, kn, v = proj[0] * q_inv, proj[1] * k_inv, proj[2]
    g = og[...]
    rows = lax.broadcasted_iota(jnp.int32, (C, C), 0)
    cols = lax.broadcasted_iota(jnp.int32, (C, C), 1)
    beta_row = 1.0 / (1.0 + jnp.exp(-bl[...]))
    beta = jnp.sum(jnp.where(rows == cols, beta_row, 0.0), axis=1, keepdims=True)
    cum = jnp.sum(jnp.where(cols <= rows, ld[...], 0.0), axis=1, keepdims=True)
    cum_row = jnp.sum(jnp.where(rows == cols, cum, 0.0), axis=0, keepdims=True)
    total = cum[C - 1 : C, :]
    decay = jnp.exp(-jnp.abs(cum - cum_row))
    opening = jnp.exp(cum)
    fading = jnp.exp(total - cum)
    causal, anti = rows >= cols, rows <= cols

    kb = kn.astype(BF16)
    qb = qn.astype(BF16)
    low = beta * jnp.where(rows > cols, decay * dot(kb, kb, 1, 1), 0.0)
    off = unit_inverse_less_identity(low, rows, cols).astype(BF16)
    bk = opening * kn
    fk = fading * kn
    x0 = beta * bk
    xs = x0 + dot(off, x0)
    xf = beta * (fk + dot(off, fk, 0, 0))
    v0 = beta * v
    w0 = v0 + dot(off, v0)
    pg = dot(jnp.where(anti, decay * dot(kb, qb, 1, 1), 0.0), g)
    y0 = beta * (pg + dot(off, pg, 0, 0))
    fk_hi, fk_lo = split(fk)
    w_hi, w_lo = split(w0)
    b_seg = dot(fk_hi, w_hi, 0, 0) + (dot(fk_lo, w_hi, 0, 0) + dot(fk_hi, w_lo, 0, 0))
    z_seg = dot(opening * qn, g, 0, 0) - dot(xs, pg, 0, 0)
    r_seg = -dot(xf, bk, 0, 0)
    a_seg = jnp.broadcast_to(jnp.exp(total), (1, DK))

    def put(ref, a, r, b, zz):
        ref[pl.ds(B_AT, DK), :] = b.astype(BF16)
        ref[pl.ds(R_AT, DK), :] = r.astype(BF16)
        ref[pl.ds(Z_AT, DK), :] = zz.astype(BF16)
        place = lax.broadcasted_iota(jnp.int32, (16, DK), 0)
        first, second, third = [t.astype(F32) for t in thirds(a)]
        tile = jnp.where(place == 0, first, jnp.where(place == 1, second, jnp.where(place == 2, third, 0.0)))
        ref[pl.ds(A_AT, 16), :] = tile.astype(BF16)

    def scale_of(ref):
        return jnp.sum(ref[pl.ds(A_AT, 16), :].astype(F32), axis=0, keepdims=True)

    put(ag.at[y], a_seg, r_seg, b_seg, z_seg)
    pl.semaphore_wait(barrier, len(peers))

    def y_copy(step, piece, up):
        slot = (y - step + Y) % Y if up else (y + step) % Y
        start, size = PIECES[piece]
        part = ag.at[slot, pl.ds(start, size)]
        ss, rs = (up_s, up_r) if up else (dn_s, dn_r)
        return pltpu.make_async_remote_copy(
            src_ref=part, dst_ref=part, send_sem=ss.at[step, piece], recv_sem=rs.at[step, piece],
            device_id=at(dy=1) if up else at(dy=-1), device_id_type=MESH,
        )

    def y_arrived(step, piece, up):
        slot = (y - step - 1 + Y) % Y if up else (y + step + 1) % Y
        start, size = PIECES[piece]
        part = ag.at[slot, pl.ds(start, size)]
        ss, rs = (up_s, up_r) if up else (dn_s, dn_r)
        pltpu.make_async_remote_copy(
            src_ref=part, dst_ref=part, send_sem=ss.at[step, piece], recv_sem=rs.at[step, piece],
            device_id=at(dy=1) if up else at(dy=-1), device_id_type=MESH,
        ).wait_recv()

    for step in range(5):
        for piece in range(3):
            for up, steps in ((True, 4), (False, 3)):
                if 1 <= step <= steps:
                    y_arrived(step - 1, piece, up)
                if step < steps:
                    y_copy(step, piece, up).start()

    fwd_a = jnp.ones((1, DK), F32)
    fwd = jnp.zeros((DK, 2 * DK), F32)
    bwd_a = jnp.ones((1, DK), F32)
    bwd = jnp.zeros((DK, 2 * DK), F32)

    def twice(row):
        return jnp.concatenate([row, row], axis=1)

    eye = (
        lax.broadcasted_iota(jnp.int32, (DK, DK), 0) == lax.broadcasted_iota(jnp.int32, (DK, DK), 1)
    ).astype(F32)
    for turn in range(Y):
        j, i = turn, Y - 1 - turn

        @pl.when(y == j)
        def _(fwd=fwd, fwd_a=fwd_a):
            pre[0] = fwd
            pre[2, 0:1, 0:DK] = fwd_a

        @pl.when(y == i)
        def _(bwd=bwd, bwd_a=bwd_a):
            pre[1] = bwd
            pre[2, 8:9, 0:DK] = bwd_a

        a_j, r_j = scale_of(ag.at[j]), ag[j, pl.ds(R_AT, DK), :]
        b_j = ag[j, pl.ds(B_AT, DK), :].astype(F32)
        fwd = (
            twice(a_j) * fwd
            + dot(r_j, fwd)
            + jnp.concatenate([fwd_a * r_j.astype(F32), b_j], axis=1)
        )
        fwd_a = fwd_a * a_j
        a_i, r_i = scale_of(ag.at[i]), ag[i, pl.ds(R_AT, DK), :]
        z_i = ag[i, pl.ds(Z_AT, DK), :].astype(F32)
        r_it = dot(r_i, eye, 0, 0)
        bwd = (
            twice(a_i) * bwd
            + dot(r_it, bwd)
            + jnp.concatenate([bwd_a * r_it, z_i], axis=1)
        )
        bwd_a = bwd_a * a_i

    put(xg.at[x], fwd_a, fwd[:, :DK], fwd[:, DK:], bwd[:, DK:])
    x_copies = []
    for m in range(1, X):
        start = pl.multiple_of(jnp.where(x + m < X, B_AT, R_AT), 128)
        part = xg.at[x, pl.ds(start, 272)]
        x_copies.append(
            pltpu.make_async_remote_copy(
                src_ref=part, dst_ref=part, send_sem=x_s.at[m], recv_sem=x_r.at[m],
                device_id=at(dx=m), device_id_type=MESH,
            )
        )
        x_copies[-1].start()
    for m in range(1, X):
        source = (x - m + X) % X
        start = pl.multiple_of(jnp.where(source < x, B_AT, R_AT), 128)
        part = xg.at[source, pl.ds(start, 272)]
        pltpu.make_async_remote_copy(
            src_ref=part, dst_ref=part, send_sem=x_s.at[m], recv_sem=x_r.at[m],
            device_id=at(dx=m), device_id_type=MESH,
        ).wait_recv()
    state, seed = fin.at[0], fin.at[1]
    state[...] = jnp.zeros((DK, DK), F32)
    seed[...] = jnp.zeros((DK, DK), F32)
    for j in range(X - 1):
        i = X - 1 - j

        @pl.when(j < x)
        def _():
            old = state[...]
            state[...] = (
                scale_of(xg.at[j]) * old
                + dot(xg[j, pl.ds(R_AT, DK), :], old)
                + xg[j, pl.ds(B_AT, DK), :].astype(F32)
            )

        @pl.when(i > x)
        def _():
            old = seed[...]
            seed[...] = (
                scale_of(xg.at[i]) * old
                + dot(xg[i, pl.ds(R_AT, DK), :], old, 0, 0)
                + xg[i, pl.ds(Z_AT, DK), :].astype(F32)
            )

    old = state[...]
    s_in = pre[2, 0:1, 0:DK] * old + dot(pre[0, :, 0:DK], old) + pre[0, :, DK : 2 * DK]
    old = seed[...]
    g_out = pre[2, 8:9, 0:DK] * old + dot(pre[1, :, 0:DK], old) + pre[1, :, DK : 2 * DK]

    w = w0 - dot(xs, s_in)
    yy = y0 + dot(xf, g_out)
    wb, yb = w.astype(BF16), yy.astype(BF16)
    s_hi, s_lo = split(s_in)
    e = jnp.where(causal, decay * dot(g, wb, 1, 1), 0.0)
    et = jnp.where(anti, decay * dot(wb, g, 1, 1), 0.0)
    h = jnp.where(rows > cols, dot(yb, wb, 1, 1), dot(wb, yb, 1, 1)) * decay
    h = jnp.where(rows == cols, 0.0, h)
    dq = opening * (dot(g, s_hi, 1, 1) + dot(g, s_lo, 1, 1)) + dot(e, kb)
    dk = fading * dot(wb, g_out, 1, 1) + dot(et, qb) - dot(h, kb) - opening * dot(yb, s_hi, 1, 1)
    dq = q_inv * (dq - qn * jnp.sum(qn * dq, axis=1, keepdims=True))
    dk = k_inv * (dk - kn * jnp.sum(kn * dk, axis=1, keepdims=True))
    grads = [split(t) for t in (dq, dk, yy)]

    order = (4, -3, 3, -2, 2, -1, 1, 0)

    def block(turn, which):
        to = ((z + order[turn] + Z) % Z) * 2 + which
        at_row = pl.multiple_of(to * DK, DK)
        total = None
        for p in range(3):
            weight = wgt[p, pl.ds(at_row, DK), :]
            for half in grads[p]:
                term = dot(half, weight, 1, 1)
                total = term if total is None else total + term
        return total

    def core_copy(turn):
        return pltpu.make_async_remote_copy(
            src_ref=core_out.at[turn], dst_ref=core_in.at[turn], send_sem=c_s.at[turn],
            recv_sem=c_r.at[turn], device_id=at(dc=1), device_id_type=MESH,
        )

    for turn in range(Z):
        core_out[turn] = block(turn, 1 - core).astype(BF16)
        core_copy(turn).start()

    def z_copy(step, up):
        src, dst, ss, rs = (up_out, up_in, zu_s, zu_r) if up else (dn_out, dn_in, zd_s, zd_r)
        return pltpu.make_async_remote_copy(
            src_ref=src.at[step], dst_ref=dst.at[step], send_sem=ss.at[step], recv_sem=rs.at[step],
            device_id=at(dz=1) if up else at(dz=-1), device_id_type=MESH,
        )

    for turn in range(Z):
        own[turn] = block(turn, core)
    for turn in range(Z):
        core_copy(turn).wait_recv()
        mine = own[turn] + core_in[turn].astype(F32)
        step, up = turn // 2, turn % 2 == 0
        if turn == Z - 1:
            z_copy(3, True).wait_recv()
            z_copy(2, False).wait_recv()
            mine = mine + up_in[3].astype(F32) + dn_in[2].astype(F32)
            out[...] = mine.astype(BF16)
            continue
        if step > 0:
            z_copy(step - 1, up).wait_recv()
            mine = mine + (up_in if up else dn_in)[step - 1].astype(F32)
        (up_out if up else dn_out)[step] = mine.astype(BF16)
        z_copy(step, up).start()

    for step in range(4):
        for piece in range(3):
            y_copy(step, piece, True).wait_send()
            if step < 3:
                y_copy(step, piece, False).wait_send()
        z_copy(step, True).wait_send()
        if step < 3:
            z_copy(step, False).wait_send()
    for copy in x_copies:
        copy.wait_send()
    for turn in range(Z):
        core_copy(turn).wait_send()


def on_device(tokens, qkv_weight, beta_logit, log_decay, out_grad):
    dma = pltpu.SemaphoreType.DMA
    return pl.pallas_call(
        kernel,
        out_shape=jax.ShapeDtypeStruct((C, DK), BF16),
        in_specs=[pl.BlockSpec(memory_space=pltpu.VMEM)] * 5,
        out_specs=pl.BlockSpec(memory_space=pltpu.VMEM),
        scratch_shapes=[
            pltpu.VMEM((Y, ROWS, DK), BF16),
            pltpu.VMEM((X, ROWS, DK), BF16),
            pltpu.VMEM((3, DK, 2 * DK), F32),
            pltpu.VMEM((Z, C, DK), BF16),
            pltpu.VMEM((Z, C, DK), BF16),
            pltpu.VMEM((Z, C, DK), F32),
            pltpu.VMEM((4, C, DK), BF16),
            pltpu.VMEM((3, C, DK), BF16),
            pltpu.VMEM((4, C, DK), BF16),
            pltpu.VMEM((3, C, DK), BF16),
            pltpu.VMEM((2, DK, DK), F32),
            dma((4, 3)), dma((4, 3)), dma((3, 3)), dma((3, 3)),
            dma((X,)), dma((X,)),
            dma((Z,)), dma((Z,)),
            dma((4,)), dma((4,)), dma((3,)), dma((3,)),
        ],
        compiler_params=pltpu.CompilerParams(
            collective_id=0, has_side_effects=True, vmem_limit_bytes=40 * 2**20
        ),
        name="delta_rule",
    )(tokens, qkv_weight, beta_logit, log_decay, out_grad)


def solution(mesh):
    return jax.shard_map(
        on_device,
        mesh=mesh,
        in_specs=(
            P("seq", None),
            P(None, None, "head"),
            P("head", "seq"),
            P("head", "seq"),
            P("seq", "head"),
        ),
        out_specs=P("seq", "head"),
        check_vma=False,
    )
```

time: 500 us -> 61.3 us (0.12)
  the two profiles are of different devices: /device:TPU:1 before, /device:TPU:64 now
where the time goes in v1:
time: 61.3 us; the launch traced here: 61.1 us
  Pallas kernels  55.6 us (91%)
  local copies, waits for them, and re-layouts  5.46 us (9%)
    pallas_call x1, Pallas kernels, on_device(): pl.pallas_call(kernel, out_shape=jax.ShapeDtypeStruct((C, DK), BF16), in_...  55.6 us
    unnamed x11, local copies, waits for them, and re-layouts  5.46 us

profile of v1, /device:TPU:64, one launch (start us, length us, event | category | flops | bytes accessed | tf_op | source)
XLA Modules:
  0.0 61.1 jit_solution(2307944240734514954)
XLA Ops:
  0.0 0.0 copy-start
  0.0 1.4 %copy-done = bf16[3,2048,128]{2,1,0:T(8,128)(2,1)S(1)} copy-done((bf16[3,2048,128]{2,1,0:T(8,128)(2,1)S(1)}, bf16[3,2048,128]{2,1,0:T(8,128)(2,1)}, u32[]{:S(2)}) %copy-start) | copy-done | bytes 1572888
  1.4 0.0 copy-start.1
  1.4 1.2 %copy-done.1 = bf16[256,2048]{1,0:T(8,128)(2,1)S(1)} copy-done((bf16[256,2048]{1,0:T(8,128)(2,1)S(1)}, bf16[256,2048]{1,0:T(8,128)(2,1)}, u32[]{:S(2)}) %copy-start.1) | copy-done | bytes 1048600
  2.6 0.0 copy-start.2
  2.6 0.8 %copy-done.2 = bf16[256,128]{1,0:T(8,128)(2,1)S(1)} copy-done((bf16[256,128]{1,0:T(8,128)(2,1)S(1)}, bf16[256,128]{1,0:T(8,128)(2,1)}, u32[]{:S(2)}) %copy-start.2) | copy-done | bytes 65560
  3.5 0.0 copy-start.3
  3.5 0.7 %copy-done.3 = f32[1,256]{1,0:T(1,128)S(1)} copy-done((f32[1,256]{1,0:T(1,128)S(1)}, f32[1,256]{1,0:T(1,128)}, u32[]{:S(2)}) %copy-start.3) | copy-done | bytes 1048
  4.2 0.0 copy-start.4
  4.2 0.7 %copy-done.4 = f32[1,256]{1,0:T(1,128)S(1)} copy-done((f32[1,256]{1,0:T(1,128)S(1)}, f32[1,256]{1,0:T(1,128)}, u32[]{:S(2)}) %copy-start.4) | copy-done | bytes 1048
  4.8 55.6 %delta_rule.1 = bf16[256,128]{1,0:T(8,128)(2,1)S(1)} custom-call(bf16[256,2048]{1,0:T(8,128)(2,1)S(1)} %copy-done.1, bf16[3,2048,128]{2,1,0:T(8,128)(2,1)S(1)} %copy-done, f32[1,256]{1,0:T(1,128)S(1)} %copy-done.3, f32[1,256]{1,0:T(1,128)S(1)} %copy-done.4, bf16[256,128]{1,0:T(8,128)(2,1)S(1)} %copy-done.2), custom_call_target="tpu_custom_call" | custom-call | tf_op jit(solution)/shard_map/delta_rule/pallas_call | solution.py:325
  60.5 0.6 %copy.7 = bf16[256,128]{1,0:T(8,128)(2,1)} copy(bf16[256,128]{1,0:T(8,128)(2,1)S(1)} %delta_rule.1) | data formatting | bytes 131072
Async XLA Ops:
  0.0 1.4 %copy-start = (bf16[3,2048,128]{2,1,0:T(8,128)(2,1)S(1)}, bf16[3,2048,128]{2,1,0:T(8,128)(2,1)}, u32[]{:S(2)}) copy-start(bf16[3,2048,128]{2,1,0:T(8,128)(2,1)} %wgt.1) | copy-start | bytes 4718596
  1.4 1.2 %copy-start.1 = (bf16[256,2048]{1,0:T(8,128)(2,1)S(1)}, bf16[256,2048]{1,0:T(8,128)(2,1)}, u32[]{:S(2)}) copy-start(bf16[256,2048]{1,0:T(8,128)(2,1)} %tok.1) | copy-start | bytes 3145732
  2.6 0.8 %copy-start.2 = (bf16[256,128]{1,0:T(8,128)(2,1)S(1)}, bf16[256,128]{1,0:T(8,128)(2,1)}, u32[]{:S(2)}) copy-start(bf16[256,128]{1,0:T(8,128)(2,1)} %og.1) | copy-start | bytes 196612
  3.5 0.7 %copy-start.3 = (f32[1,256]{1,0:T(1,128)S(1)}, f32[1,256]{1,0:T(1,128)}, u32[]{:S(2)}) copy-start(f32[1,256]{1,0:T(1,128)} %bl.1) | copy-start | bytes 3076
  4.2 0.7 %copy-start.4 = (f32[1,256]{1,0:T(1,128)S(1)}, f32[1,256]{1,0:T(1,128)}, u32[]{:S(2)}) copy-start(f32[1,256]{1,0:T(1,128)} %ld.1) | copy-start | bytes 3076

commit v2 on v1

v2 whole, which is shorter than its diff:
```python
import functools

import jax
import jax.numpy as jnp
from jax import lax
from jax.experimental import pallas as pl
from jax.experimental.pallas import tpu as pltpu
from jax.sharding import PartitionSpec as P

F32 = jnp.float32
BF16 = jnp.bfloat16
MESH = pl.DeviceIdType.MESH
X, Y, Z = 4, 8, 8
C, DK = 256, 128
B_AT, R_AT, A_AT, Z_AT, ROWS = 0, 128, 256, 272, 400
PIECES = ((R_AT, 144), (B_AT, 128), (Z_AT, 128))
FAR = ((0, 208), (208, 192))
K_PARTS, K_PART = 4, 512
HALVES, H_ROWS = 2, 128


def dot(a, b, ca=1, cb=0):
    return lax.dot_general(
        a.astype(BF16), b.astype(BF16), (((ca,), (cb,)), ((), ())), preferred_element_type=F32
    )


def split(a):
    upper = a.astype(BF16)
    return upper, (a - upper.astype(F32)).astype(BF16)


def thirds(a):
    upper, rest = split(a)
    middle = rest
    lower = (a - upper.astype(F32) - middle.astype(F32)).astype(BF16)
    return upper, middle, lower


def unit_inverse_less_identity(low, rows, cols):
    def same(shift):
        return (rows >> shift) == (cols >> shift)

    power = jnp.where(same(5), low, 0.0)
    off = -power
    for _ in range(4):
        power = dot(power, power)
        off = off + power + dot(off, power)
    for shift in (5, 6, 7):
        inside = jnp.where(same(shift + 1) & ~same(shift), low, 0.0)
        left = inside + dot(off, inside)
        off = off - left - dot(left, off)
    return off


def kernel(
    tok_hbm, wgt_hbm, bl_hbm, ld_hbm, og_hbm, out,
    tok, wgt, bl, ld, og, ag, xg, core_out, core_in, own, up_out, dn_out, up_in, dn_in,
    in_sem, w_sem, up_s, up_r, dn_s, dn_r, far_s, far_r, x_s, x_r, c_s, c_r, zu_s, zu_r, zd_s, zd_r,
):
    seq, head = lax.axis_index("seq"), lax.axis_index("head")
    x, y = seq // Y, seq % Y
    z, core = head // 2, head % 2

    def at(dx=0, dy=0, dz=0, dc=0):
        return (
            ((x + dx) % X) * Y + (y + dy + Y) % Y,
            ((z + dz + Z) % Z) * 2 + (core + dc) % 2,
        )

    small = [
        pltpu.make_async_copy(src, dst, in_sem.at[i])
        for i, (src, dst) in enumerate(((ld_hbm, ld), (bl_hbm, bl), (og_hbm, og)))
    ]
    parts = []
    for k in range(K_PARTS):
        rows_k = pl.ds(k * K_PART, K_PART)
        parts.append(
            [pltpu.make_async_copy(tok_hbm.at[:, rows_k], tok.at[:, rows_k], in_sem.at[3 + k])]
            + [
                pltpu.make_async_copy(
                    wgt_hbm.at[p, rows_k, :], wgt.at[rows_k, pl.ds(p * DK, DK)], w_sem.at[k, p]
                )
                for p in range(3)
            ]
        )
    for copy in small[:2] + sum(parts, []) + small[2:]:
        copy.start()
    peers = [at(dy=1), at(dy=-1), at(dx=1), at(dx=2), at(dx=3), at(dc=1), at(dz=1), at(dz=-1)]
    barrier = pltpu.get_barrier_semaphore()
    for peer in peers:
        pl.semaphore_signal(barrier, inc=1, device_id=peer, device_id_type=MESH)

    rows = lax.broadcasted_iota(jnp.int32, (C, C), 0)
    cols = lax.broadcasted_iota(jnp.int32, (C, C), 1)
    causal, anti = rows >= cols, rows <= cols
    small[0].wait()
    small[1].wait()
    beta_row = 1.0 / (1.0 + jnp.exp(-bl[...]))
    beta = jnp.sum(jnp.where(rows == cols, beta_row, 0.0), axis=1, keepdims=True)
    cum = jnp.sum(jnp.where(cols <= rows, ld[...], 0.0), axis=1, keepdims=True)
    cum_row = jnp.sum(jnp.where(rows == cols, cum, 0.0), axis=0, keepdims=True)
    total = cum[C - 1 : C, :]
    decay = jnp.exp(-jnp.abs(cum - cum_row))
    opening = jnp.exp(cum)
    fading = jnp.exp(total - cum)

    proj = None
    for k in range(K_PARTS):
        for copy in parts[k]:
            copy.wait()
        rows_k = pl.ds(k * K_PART, K_PART)
        term = jnp.dot(tok[:, rows_k], wgt[rows_k, :], preferred_element_type=F32)
        proj = term if proj is None else proj + term
    small[2].wait()
    q, key, v = proj[:, :DK], proj[:, DK : 2 * DK], proj[:, 2 * DK :]
    q_inv = lax.rsqrt(jnp.sum(q * q, axis=1, keepdims=True) + 1e-6)
    k_inv = lax.rsqrt(jnp.sum(key * key, axis=1, keepdims=True) + 1e-6)
    qn, kn = q * q_inv, key * k_inv
    g = og[...]

    kb = kn.astype(BF16)
    qb = qn.astype(BF16)
    low = beta * jnp.where(rows > cols, decay * dot(kb, kb, 1, 1), 0.0)
    off = unit_inverse_less_identity(low, rows, cols).astype(BF16)
    bk = opening * kn
    fk = fading * kn
    x0 = beta * bk
    xs = x0 + dot(off, x0)
    xf = beta * (fk + dot(off, fk, 0, 0))
    v0 = beta * v
    w0 = v0 + dot(off, v0)
    pg = dot(jnp.where(anti, decay * dot(kb, qb, 1, 1), 0.0), g)
    y0 = beta * (pg + dot(off, pg, 0, 0))
    fk_hi, fk_lo = split(fk)
    w_hi, w_lo = split(w0)
    b_seg = dot(fk_hi, w_hi, 0, 0) + (dot(fk_lo, w_hi, 0, 0) + dot(fk_hi, w_lo, 0, 0))
    z_seg = dot(opening * qn, g, 0, 0) - dot(xs, pg, 0, 0)
    r_seg = -dot(xf, bk, 0, 0)
    a_seg = jnp.broadcast_to(jnp.exp(total), (1, DK))

    def put(ref, a, r, b, zz):
        ref[pl.ds(B_AT, DK), :] = b.astype(BF16)
        ref[pl.ds(R_AT, DK), :] = r.astype(BF16)
        ref[pl.ds(Z_AT, DK), :] = zz.astype(BF16)
        place = lax.broadcasted_iota(jnp.int32, (16, DK), 0)
        first, second, third = [t.astype(F32) for t in thirds(a)]
        tile = jnp.where(place == 0, first, jnp.where(place == 1, second, jnp.where(place == 2, third, 0.0)))
        ref[pl.ds(A_AT, 16), :] = tile.astype(BF16)

    def scale_of(ref):
        return jnp.sum(ref[pl.ds(A_AT, 16), :].astype(F32), axis=0, keepdims=True)

    put(ag.at[y], a_seg, r_seg, b_seg, z_seg)
    pl.semaphore_wait(barrier, len(peers))

    def y_copy(step, piece, up):
        slot = (y - step + Y) % Y if up else (y + step) % Y
        if step < 3:
            start, size = PIECES[piece]
            ss, rs = (up_s, up_r) if up else (dn_s, dn_r)
            ss, rs = ss.at[step, piece], rs.at[step, piece]
        else:
            start, size = FAR[0 if up else 1]
            ss, rs = far_s.at[0 if up else 1], far_r.at[0 if up else 1]
        part = ag.at[slot, pl.ds(start, size)]
        return pltpu.make_async_remote_copy(
            src_ref=part, dst_ref=part, send_sem=ss, recv_sem=rs,
            device_id=at(dy=1) if up else at(dy=-1), device_id_type=MESH,
        )

    def y_arrived(step, piece, up):
        slot = (y - step - 1 + Y) % Y if up else (y + step + 1) % Y
        if step < 3:
            start, size = PIECES[piece]
            ss, rs = (up_s, up_r) if up else (dn_s, dn_r)
            ss, rs = ss.at[step, piece], rs.at[step, piece]
        else:
            start, size = FAR[0 if up else 1]
            ss, rs = far_s.at[0 if up else 1], far_r.at[0 if up else 1]
        part = ag.at[slot, pl.ds(start, size)]
        pltpu.make_async_remote_copy(
            src_ref=part, dst_ref=part, send_sem=ss, recv_sem=rs,
            device_id=at(dy=1) if up else at(dy=-1), device_id_type=MESH,
        ).wait_recv()

    for step in range(4):
        for piece in range(3):
            for up in (True, False):
                if step > 0:
                    y_arrived(step - 1, piece, up)
                if step < 3:
                    y_copy(step, piece, up).start()
                elif piece == (1 if up else 2):
                    y_copy(3, 0, up).start()
    y_arrived(3, 0, True)
    y_arrived(3, 0, False)

    def leaf(slot):
        r = ag[slot, pl.ds(R_AT, DK), :].astype(F32)
        return (
            scale_of(ag.at[slot]), r, r.T,
            ag[slot, pl.ds(B_AT, DK), :].astype(F32), ag[slot, pl.ds(Z_AT, DK), :].astype(F32),
        )

    def wide(left, right):
        return jnp.concatenate([left, right], axis=1)

    def ahead(early, late):
        a0, r0, _, b0, _ = early
        a1, r1, _, b1, _ = late
        both = dot(r1, wide(r0, b0))
        return a0 * a1, a1 * r0 + a0 * r1 + both[:, :DK], a1 * b0 + b1 + both[:, DK:]

    def behind(early, late):
        a0, _, t0, _, z0 = early
        a1, _, t1, _, z1 = late
        both = dot(t0, wide(t1, z1))
        return a0 * a1, a1 * t0 + a0 * t1 + both[:, :DK], a0 * z1 + z0 + both[:, DK:]

    def compose(early, late):
        a, r, b = ahead(early, late)
        _, t, zz = behind(early, late)
        return a, r, t, b, zz

    def pick(flag, one, other):
        return tuple(jnp.where(flag, p, o) for p, o in zip(one, other))

    leaves = [leaf(j) for j in range(Y)]
    pairs = [compose(leaves[2 * j], leaves[2 * j + 1]) for j in range(4)]
    quads = [compose(pairs[0], pairs[1]), compose(pairs[2], pairs[3])]
    a_row, r_row, b_row = ahead(quads[0], quads[1])
    _, _, z_row = behind(quads[0], quads[1])

    put(xg.at[x], a_row, r_row, b_row, z_row)
    x_copies = []
    for m in (2, 1, 3):
        start = pl.multiple_of(jnp.where(x + m < X, B_AT, R_AT), 128)
        part = xg.at[x, pl.ds(start, 272)]
        x_copies.append(
            pltpu.make_async_remote_copy(
                src_ref=part, dst_ref=part, send_sem=x_s.at[m], recv_sem=x_r.at[m],
                device_id=at(dx=m), device_id_type=MESH,
            )
        )
        x_copies[-1].start()

    zero = jnp.zeros((DK, DK), F32)
    none = (jnp.ones((1, DK), F32), zero, zero, zero, zero)
    four, two, one = y >= 4, y % 4 >= 2, y % 2 == 1
    before = pick(four, quads[0], none)
    second = pick(two, pick(four, pairs[2], pairs[0]), none)
    third = pick(one, leaf(y - y % 2), none)
    a_pre, r_pre, b_pre = ahead(before, second)
    a_pre, r_pre, b_pre = ahead((a_pre, r_pre, None, b_pre, None), third)
    first = pick(one, none, leaf(y + 1 - y % 2))
    second = pick(two, none, pick(four, pairs[3], pairs[1]))
    last = pick(four, none, quads[1])
    a_suf, t_suf, z_suf = behind(second, last)
    a_suf, t_suf, z_suf = behind(first, (a_suf, None, t_suf, None, z_suf))

    for m in (1, 3, 2):
        source = (x - m + X) % X
        start = pl.multiple_of(jnp.where(source < x, B_AT, R_AT), 128)
        part = xg.at[source, pl.ds(start, 272)]
        pltpu.make_async_remote_copy(
            src_ref=part, dst_ref=part, send_sem=x_s.at[m], recv_sem=x_r.at[m],
            device_id=at(dx=m), device_id_type=MESH,
        ).wait_recv()
    state, seed = zero, zero
    for j in range(X - 1):
        i = X - 1 - j
        r_j, r_i = xg[j, pl.ds(R_AT, DK), :], xg[i, pl.ds(R_AT, DK), :]
        grown = xg[j, pl.ds(B_AT, DK), :].astype(F32)
        if j:
            grown = grown + scale_of(xg.at[j]) * state + dot(r_j, state)
        state = jnp.where(j < x, grown, state)
        grown = xg[i, pl.ds(Z_AT, DK), :].astype(F32)
        if j:
            grown = grown + scale_of(xg.at[i]) * seed + dot(r_i, seed, 0, 0)
        seed = jnp.where(i > x, grown, seed)
    s_in = a_pre * state + dot(r_pre, state) + b_pre
    g_out = a_suf * seed + dot(t_suf, seed) + z_suf

    w = w0 - dot(xs, s_in)
    yy = y0 + dot(xf, g_out)
    wb, yb = w.astype(BF16), yy.astype(BF16)
    s_hi, s_lo = split(s_in)
    e = jnp.where(causal, decay * dot(g, wb, 1, 1), 0.0)
    et = jnp.where(anti, decay * dot(wb, g, 1, 1), 0.0)
    h = jnp.where(rows > cols, dot(yb, wb, 1, 1), dot(wb, yb, 1, 1)) * decay
    h = jnp.where(rows == cols, 0.0, h)
    dq = opening * (dot(g, s_hi, 1, 1) + dot(g, s_lo, 1, 1)) + dot(e, kb)
    dk = fading * dot(wb, g_out, 1, 1) + dot(et, qb) - dot(h, kb) - opening * dot(yb, s_hi, 1, 1)
    dq = q_inv * (dq - qn * jnp.sum(qn * dq, axis=1, keepdims=True))
    dk = k_inv * (dk - kn * jnp.sum(kn * dk, axis=1, keepdims=True))
    grads_hi, grads_lo = split(jnp.concatenate([dq, dk, yy], axis=1))

    order = (4, -3, 3, -2, 2, -1, 1, 0)

    def core_copy(turn):
        return pltpu.make_async_remote_copy(
            src_ref=core_out.at[turn], dst_ref=core_in.at[turn], send_sem=c_s.at[turn],
            recv_sem=c_r.at[turn], device_id=at(dc=1), device_id_type=MESH,
        )

    def product(turn):
        to = pl.multiple_of(((z + order[turn] + Z) % Z) * 2 * DK, 2 * DK)
        weight = wgt[pl.ds(to, 2 * DK), :]
        both = dot(grads_hi, weight, 1, 1) + dot(grads_lo, weight, 1, 1)
        left, right = both[:, :DK], both[:, DK:]
        core_out[turn] = jnp.where(core == 0, right, left).astype(BF16)
        core_copy(turn).start()
        own[turn] = jnp.where(core == 0, left, right)

    def z_copy(step, half, up):
        src, dst, ss, rs = (up_out, up_in, zu_s, zu_r) if up else (dn_out, dn_in, zd_s, zd_r)
        part = pl.ds(half * H_ROWS, H_ROWS)
        return pltpu.make_async_remote_copy(
            src_ref=src.at[step, part], dst_ref=dst.at[step, part], send_sem=ss.at[step, half],
            recv_sem=rs.at[step, half], device_id=at(dz=1) if up else at(dz=-1), device_id_type=MESH,
        )

    def pass_on(step):
        turns = [(2 * step, True)] + ([(2 * step + 1, False)] if step < 3 else [])
        for turn, up in turns:
            core_copy(turn).wait_recv()
        for half in range(HALVES):
            part = pl.ds(half * H_ROWS, H_ROWS)
            for turn, up in turns:
                mine = own[turn, part, :] + core_in[turn, part, :].astype(F32)
                if step:
                    z_copy(step - 1, half, up).wait_recv()
                    mine = mine + (up_in if up else dn_in)[step - 1, part, :].astype(F32)
                (up_out if up else dn_out)[step, part, :] = mine.astype(BF16)
                z_copy(step, half, up).start()

    for turn in range(4):
        product(turn)
    pass_on(0)
    for turn in range(4, Z):
        product(turn)
    for step in range(1, 4):
        pass_on(step)
    core_copy(Z - 1).wait_recv()
    for half in range(HALVES):
        part = pl.ds(half * H_ROWS, H_ROWS)
        mine = own[Z - 1, part, :] + core_in[Z - 1, part, :].astype(F32)
        z_copy(2, half, False).wait_recv()
        mine = mine + dn_in[2, part, :].astype(F32)
        z_copy(3, half, True).wait_recv()
        out[part, :] = (mine + up_in[3, part, :].astype(F32)).astype(BF16)

    for step in range(4):
        for piece in range(3 if step < 3 else 1):
            y_copy(step, piece, True).wait_send()
            y_copy(step, piece, False).wait_send()
        for half in range(HALVES):
            z_copy(step, half, True).wait_send()
            if step < 3:
                z_copy(step, half, False).wait_send()
    for copy in x_copies:
        copy.wait_send()
    for turn in range(Z):
        core_copy(turn).wait_send()


def on_device(tokens, qkv_weight, beta_logit, log_decay, out_grad):
    dma = pltpu.SemaphoreType.DMA
    return pl.pallas_call(
        kernel,
        out_shape=jax.ShapeDtypeStruct((C, DK), BF16),
        in_specs=[pl.BlockSpec(memory_space=pl.ANY)] * 5,
        out_specs=pl.BlockSpec(memory_space=pltpu.VMEM),
        scratch_shapes=[
            pltpu.VMEM((C, K_PARTS * K_PART), BF16),
            pltpu.VMEM((K_PARTS * K_PART, 3 * DK), BF16),
            pltpu.VMEM((1, C), F32),
            pltpu.VMEM((1, C), F32),
            pltpu.VMEM((C, DK), BF16),
            pltpu.VMEM((Y, ROWS, DK), BF16),
            pltpu.VMEM((X, ROWS, DK), BF16),
            pltpu.VMEM((Z, C, DK), BF16),
            pltpu.VMEM((Z, C, DK), BF16),
            pltpu.VMEM((Z, C, DK), F32),
            pltpu.VMEM((4, C, DK), BF16),
            pltpu.VMEM((3, C, DK), BF16),
            pltpu.VMEM((4, C, DK), BF16),
            pltpu.VMEM((3, C, DK), BF16),
            dma((3 + K_PARTS,)), dma((K_PARTS, 3)),
            dma((3, 3)), dma((3, 3)), dma((3, 3)), dma((3, 3)), dma((2,)), dma((2,)),
            dma((X,)), dma((X,)),
            dma((Z,)), dma((Z,)),
            dma((4, HALVES)), dma((4, HALVES)), dma((3, HALVES)), dma((3, HALVES)),
        ],
        compiler_params=pltpu.CompilerParams(
            collective_id=0, has_side_effects=True, vmem_limit_bytes=63 * 2**20
        ),
        name="delta_rule",
    )(tokens, qkv_weight, beta_logit, log_decay, out_grad)


def solution(mesh):
    return jax.shard_map(
        on_device,
        mesh=mesh,
        in_specs=(
            P("seq", None),
            P(None, None, "head"),
            P("head", "seq"),
            P("head", "seq"),
            P("seq", "head"),
        ),
        out_specs=P("seq", "head"),
        check_vma=False,
    )
```

time: 61.3 us -> 55.8 us (0.910)
  local copies, waits for them, and re-layouts: 5.46 us -> 1.47 us
  Pallas kernels: 55.6 us -> 54.1 us
    unnamed x11 -> x1, local copies, waits for them, and re-layouts: 5.46 us -> 1.47 us
    pallas_call x1, Pallas kernels: 55.6 us -> 54.1 us  [on_device(): pl.pallas_call(kernel, out_shape=jax.ShapeDtypeStruct((C, DK), BF16), in_...]
where the time goes in v2:
time: 55.8 us; the launch traced here: 55.6 us
  Pallas kernels  54.1 us (97%)
  local copies, waits for them, and re-layouts  1.47 us (3%)
    pallas_call x1, Pallas kernels, on_device(): pl.pallas_call(kernel, out_shape=jax.ShapeDtypeStruct((C, DK), BF16), in_...  54.1 us
    unnamed x1, local copies, waits for them, and re-layouts  1.47 us

profile of v2, /device:TPU:64, one launch (start us, length us, event | category | flops | bytes accessed | tf_op | source)
XLA Modules:
  0.0 55.6 jit_solution(1080874640038913051)
XLA Ops:
  0.0 54.1 %delta_rule.1 = bf16[256,128]{1,0:T(8,128)(2,1)} custom-call(bf16[256,2048]{1,0:T(8,128)(2,1)} %tok_hbm.1, bf16[3,2048,128]{2,1,0:T(8,128)(2,1)} %wgt_hbm.1, f32[1,256]{1,0:T(1,128)} %bl_hbm.1, f32[1,256]{1,0:T(1,128)} %ld_hbm.1, bf16[256,128]{1,0:T(8,128)(2,1)} %og_hbm.1), custom_call_target="tpu_custom_call" | custom-call | tf_op jit(solution)/shard_map/delta_rule/pallas_call | solution.py:370
  54.1 1.5 %copy.7 = bf16[256,128]{1,0:T(8,128)(2,1)} copy(bf16[256,128]{1,0:T(8,128)(2,1)} %delta_rule.1) | data formatting | bytes 131072

commit v3 on v2

v3 whole, which is shorter than its diff:
```python
import functools

import jax
import jax.numpy as jnp
from jax import lax
from jax.experimental import pallas as pl
from jax.experimental.pallas import tpu as pltpu
from jax.sharding import PartitionSpec as P

F32 = jnp.float32
BF16 = jnp.bfloat16
MESH = pl.DeviceIdType.MESH
X, Y, Z = 4, 8, 8
C, DK = 256, 128
B_AT, R_AT, A_AT, Z_AT, ROWS = 0, 128, 256, 272, 400
PIECES = ((R_AT, 144), (B_AT, 128), (Z_AT, 128))
K_PARTS, K_PART = 2, 1024
ORDER = (4, -3, 3, -2, 2, -1, 1, 0)
LAG = 3


def dot(a, b, ca=1, cb=0):
    return lax.dot_general(
        a.astype(BF16), b.astype(BF16), (((ca,), (cb,)), ((), ())), preferred_element_type=F32
    )


def split(a):
    upper = a.astype(BF16)
    return upper, (a - upper.astype(F32)).astype(BF16)


def thirds(a):
    upper, rest = split(a)
    middle = rest
    lower = (a - upper.astype(F32) - middle.astype(F32)).astype(BF16)
    return upper, middle, lower


def unit_inverse_less_identity(low, rows, cols):
    def same(shift):
        return (rows >> shift) == (cols >> shift)

    power = jnp.where(same(5), low, 0.0)
    off = -power
    for _ in range(4):
        power = dot(power, power)
        off = off + power + dot(off, power)
    for shift in (5, 6, 7):
        inside = jnp.where(same(shift + 1) & ~same(shift), low, 0.0)
        left = inside + dot(off, inside)
        off = off - left - dot(left, off)
    return off


def kernel(
    tok_hbm, wgt_hbm, bl_hbm, ld_hbm, og_hbm, out,
    tok, wgt, bl, ld, og, ag, qg, xg, core_out, core_in, own, z_out, z_in,
    in_sem, w_sem, a_s, a_r, q_s, q_r, x_s, x_r, c_s, c_r, z_s, z_r,
):
    seq, head = lax.axis_index("seq"), lax.axis_index("head")
    x, y = seq // Y, seq % Y
    z, core = head // 2, head % 2

    def at(dx=0, dy=0, dz=0, dc=0):
        return (
            ((x + dx) % X) * Y + (y + dy + Y) % Y,
            ((z + dz + Z) % Z) * 2 + (core + dc) % 2,
        )

    small = [
        pltpu.make_async_copy(src, dst, in_sem.at[i])
        for i, (src, dst) in enumerate(((ld_hbm, ld), (bl_hbm, bl), (og_hbm, og)))
    ]
    parts = []
    for k in range(K_PARTS):
        rows_k = pl.ds(k * K_PART, K_PART)
        parts.append(
            [pltpu.make_async_copy(tok_hbm.at[:, rows_k], tok.at[:, rows_k], in_sem.at[3 + k])]
            + [
                pltpu.make_async_copy(
                    wgt_hbm.at[p, rows_k, :], wgt.at[p, rows_k, :], w_sem.at[k, p]
                )
                for p in range(3)
            ]
        )
    for copy in small[:2] + sum(parts, []) + small[2:]:
        copy.start()
    pair, odd = y // 2, y % 2
    way = 2 * odd - 1
    peers = [at(dy=m * way) for m in (-2, -1, 1, 2, 3)]
    peers += [at(dx=m) for m in (1, 2, 3)] + [at(dc=1)] + [at(dz=m) for m in range(1, Z)]
    barrier = pltpu.get_barrier_semaphore()
    for peer in peers:
        pl.semaphore_signal(barrier, inc=1, device_id=peer, device_id_type=MESH)

    rows = lax.broadcasted_iota(jnp.int32, (C, C), 0)
    cols = lax.broadcasted_iota(jnp.int32, (C, C), 1)
    causal, anti = rows >= cols, rows <= cols
    small[0].wait()
    small[1].wait()
    beta_row = 1.0 / (1.0 + jnp.exp(-bl[...]))
    beta = jnp.sum(jnp.where(rows == cols, beta_row, 0.0), axis=1, keepdims=True)
    cum = jnp.sum(jnp.where(cols <= rows, ld[...], 0.0), axis=1, keepdims=True)
    cum_row = jnp.sum(jnp.where(rows == cols, cum, 0.0), axis=0, keepdims=True)
    total = cum[C - 1 : C, :]
    decay = jnp.exp(-jnp.abs(cum - cum_row))
    opening = jnp.exp(cum)
    fading = jnp.exp(total - cum)

    def weights(at_rows):
        return jnp.concatenate([wgt[p, at_rows, :] for p in range(3)], axis=1)

    proj = None
    for k in range(K_PARTS):
        for copy in parts[k]:
            copy.wait()
        rows_k = pl.ds(k * K_PART, K_PART)
        term = jnp.dot(tok[:, rows_k], weights(rows_k), preferred_element_type=F32)
        proj = term if proj is None else proj + term
    small[2].wait()
    q, key, v = proj[:, :DK], proj[:, DK : 2 * DK], proj[:, 2 * DK :]
    q_inv = lax.rsqrt(jnp.sum(q * q, axis=1, keepdims=True) + 1e-6)
    k_inv = lax.rsqrt(jnp.sum(key * key, axis=1, keepdims=True) + 1e-6)
    qn, kn = q * q_inv, key * k_inv
    g = og[...]

    kb = kn.astype(BF16)
    qb = qn.astype(BF16)
    low = beta * jnp.where(rows > cols, decay * dot(kb, kb, 1, 1), 0.0)
    off = unit_inverse_less_identity(low, rows, cols).astype(BF16)
    bk = opening * kn
    fk = fading * kn
    x0 = beta * bk
    xs = x0 + dot(off, x0)
    xf = beta * (fk + dot(off, fk, 0, 0))
    r_seg = -dot(xf, bk, 0, 0)
    a_seg = jnp.broadcast_to(jnp.exp(total), (1, DK))

    def put_r(ref, a, r):
        ref[pl.ds(R_AT, DK), :] = r.astype(BF16)
        place = lax.broadcasted_iota(jnp.int32, (16, DK), 0)
        first, second, third = [t.astype(F32) for t in thirds(a)]
        tile = jnp.where(place == 0, first, jnp.where(place == 1, second, jnp.where(place == 2, third, 0.0)))
        ref[pl.ds(A_AT, 16), :] = tile.astype(BF16)

    def put(ref, a, r, b, zz):
        put_r(ref, a, r)
        ref[pl.ds(B_AT, DK), :] = b.astype(BF16)
        ref[pl.ds(Z_AT, DK), :] = zz.astype(BF16)

    def scale_of(ref):
        return jnp.sum(ref[pl.ds(A_AT, 16), :].astype(F32), axis=0, keepdims=True)

    def pair_copy(piece, slot):
        start, size = PIECES[piece]
        part = ag.at[slot, pl.ds(start, size)]
        return pltpu.make_async_remote_copy(
            src_ref=part, dst_ref=part, send_sem=a_s.at[piece], recv_sem=a_r.at[piece],
            device_id=at(dy=-way), device_id_type=MESH,
        )

    put_r(ag.at[odd], a_seg, r_seg)
    pl.semaphore_wait(barrier, len(peers))
    pair_copy(0, odd).start()
    v0 = beta * v
    w0 = v0 + dot(off, v0)
    fk_hi, fk_lo = split(fk)
    w_hi, w_lo = split(w0)
    b_seg = dot(fk_hi, w_hi, 0, 0) + (dot(fk_lo, w_hi, 0, 0) + dot(fk_hi, w_lo, 0, 0))
    ag[odd, pl.ds(B_AT, DK), :] = b_seg.astype(BF16)
    pair_copy(1, odd).start()
    pg = dot(jnp.where(anti, decay * dot(kb, qb, 1, 1), 0.0), g)
    z_seg = dot(opening * qn, g, 0, 0) - dot(xs, pg, 0, 0)
    ag[odd, pl.ds(Z_AT, DK), :] = z_seg.astype(BF16)
    pair_copy(2, odd).start()
    y0 = beta * (pg + dot(off, pg, 0, 0))

    def leaf(ref):
        r = ref[pl.ds(R_AT, DK), :].astype(F32)
        return (
            scale_of(ref), r, r.T, ref[pl.ds(B_AT, DK), :].astype(F32), ref[pl.ds(Z_AT, DK), :].astype(F32)
        )

    def wide(left, right):
        return jnp.concatenate([left, right], axis=1)

    def ahead(early, late):
        a0, r0, _, b0, _ = early
        a1, r1, _, b1, _ = late
        both = dot(r1, wide(r0, b0))
        return a0 * a1, a1 * r0 + a0 * r1 + both[:, :DK], a1 * b0 + b1 + both[:, DK:]

    def behind(early, late):
        a0, _, t0, _, z0 = early
        a1, _, t1, _, z1 = late
        both = dot(t0, wide(t1, z1))
        return a0 * a1, a1 * t0 + a0 * t1 + both[:, :DK], a0 * z1 + z0 + both[:, DK:]

    def compose(early, late):
        a, r, b = ahead(early, late)
        _, t, zz = behind(early, late)
        return a, r, t, b, zz

    def pick(flag, one, other):
        return tuple(jnp.where(flag, p, o) for p, o in zip(one, other))

    for piece in range(3):
        pair_copy(piece, 1 - odd).wait_recv()
    early, late = leaf(ag.at[0]), leaf(ag.at[1])
    a_pair, r_pair, b_pair = ahead(early, late)
    _, _, z_pair = behind(early, late)

    put(qg.at[pair], a_pair, r_pair, b_pair, z_pair)

    def row_copy(m, slot):
        part = qg.at[slot]
        return pltpu.make_async_remote_copy(
            src_ref=part, dst_ref=part, send_sem=q_s.at[m], recv_sem=q_r.at[m],
            device_id=at(dy=m * way), device_id_type=MESH,
        )

    for m in (3, 2, 1):
        row_copy(m, pair).start()
    for m, shift in ((1, way), (2, -way), (3, 2)):
        row_copy(m, (pair + shift + 4) % 4).wait_recv()
    pairs = [leaf(qg.at[j]) for j in range(4)]
    quads = [compose(pairs[0], pairs[1]), compose(pairs[2], pairs[3])]
    a_row, r_row, b_row = ahead(quads[0], quads[1])
    _, _, z_row = behind(quads[0], quads[1])

    put(xg.at[x], a_row, r_row, b_row, z_row)
    x_copies = []
    for m in (2, 1, 3):
        start = pl.multiple_of(jnp.where(x + m < X, B_AT, R_AT), 128)
        part = xg.at[x, pl.ds(start, 272)]
        x_copies.append(
            pltpu.make_async_remote_copy(
                src_ref=part, dst_ref=part, send_sem=x_s.at[m], recv_sem=x_r.at[m],
                device_id=at(dx=m), device_id_type=MESH,
            )
        )
        x_copies[-1].start()

    zero = jnp.zeros((DK, DK), F32)
    none = (jnp.ones((1, DK), F32), zero, zero, zero, zero)
    four, two, one = y >= 4, y % 4 >= 2, y % 2 == 1
    before = pick(four, quads[0], none)
    second = pick(two, pick(four, pairs[2], pairs[0]), none)
    third = pick(one, early, none)
    a_pre, r_pre, b_pre = ahead(before, second)
    a_pre, r_pre, b_pre = ahead((a_pre, r_pre, None, b_pre, None), third)
    first = pick(one, none, late)
    second = pick(two, none, pick(four, pairs[3], pairs[1]))
    last = pick(four, none, quads[1])
    a_suf, t_suf, z_suf = behind(second, last)
    a_suf, t_suf, z_suf = behind(first, (a_suf, None, t_suf, None, z_suf))

    for m in (1, 3, 2):
        source = (x - m + X) % X
        start = pl.multiple_of(jnp.where(source < x, B_AT, R_AT), 128)
        part = xg.at[source, pl.ds(start, 272)]
        pltpu.make_async_remote_copy(
            src_ref=part, dst_ref=part, send_sem=x_s.at[m], recv_sem=x_r.at[m],
            device_id=at(dx=m), device_id_type=MESH,
        ).wait_recv()
    state, seed = zero, zero
    for j in range(X - 1):
        i = X - 1 - j
        r_j, r_i = xg[j, pl.ds(R_AT, DK), :], xg[i, pl.ds(R_AT, DK), :]
        grown = xg[j, pl.ds(B_AT, DK), :].astype(F32)
        if j:
            grown = grown + scale_of(xg.at[j]) * state + dot(r_j, state)
        state = jnp.where(j < x, grown, state)
        grown = xg[i, pl.ds(Z_AT, DK), :].astype(F32)
        if j:
            grown = grown + scale_of(xg.at[i]) * seed + dot(r_i, seed, 0, 0)
        seed = jnp.where(i > x, grown, seed)
    s_in = a_pre * state + dot(r_pre, state) + b_pre
    g_out = a_suf * seed + dot(t_suf, seed) + z_suf

    w = w0 - dot(xs, s_in)
    yy = y0 + dot(xf, g_out)
    wb, yb = w.astype(BF16), yy.astype(BF16)
    s_hi, s_lo = split(s_in)
    e = jnp.where(causal, decay * dot(g, wb, 1, 1), 0.0)
    et = jnp.where(anti, decay * dot(wb, g, 1, 1), 0.0)
    h = jnp.where(rows > cols, dot(yb, wb, 1, 1), dot(wb, yb, 1, 1)) * decay
    h = jnp.where(rows == cols, 0.0, h)
    dq = opening * (dot(g, s_hi, 1, 1) + dot(g, s_lo, 1, 1)) + dot(e, kb)
    dk = fading * dot(wb, g_out, 1, 1) + dot(et, qb) - dot(h, kb) - opening * dot(yb, s_hi, 1, 1)
    dq = q_inv * (dq - qn * jnp.sum(qn * dq, axis=1, keepdims=True))
    dk = k_inv * (dk - kn * jnp.sum(kn * dk, axis=1, keepdims=True))
    grads_hi, grads_lo = split(jnp.concatenate([dq, dk, yy], axis=1))

    def core_copy(turn):
        return pltpu.make_async_remote_copy(
            src_ref=core_out.at[turn], dst_ref=core_in.at[turn], send_sem=c_s.at[turn],
            recv_sem=c_r.at[turn], device_id=at(dc=1), device_id_type=MESH,
        )

    def z_copy(turn):
        return pltpu.make_async_remote_copy(
            src_ref=z_out.at[turn], dst_ref=z_in.at[turn], send_sem=z_s.at[turn],
            recv_sem=z_r.at[turn], device_id=at(dz=ORDER[turn]), device_id_type=MESH,
        )

    def product(turn):
        to = pl.multiple_of(((z + ORDER[turn] + Z) % Z) * 2 * DK, 2 * DK)
        weight = weights(pl.ds(to, 2 * DK))
        both = dot(grads_hi, weight, 1, 1) + dot(grads_lo, weight, 1, 1)
        left, right = both[:, :DK], both[:, DK:]
        core_out[turn] = jnp.where(core == 0, right, left).astype(BF16)
        core_copy(turn).start()
        own[turn] = jnp.where(core == 0, left, right)

    def pass_on(turn):
        core_copy(turn).wait_recv()
        z_out[turn] = (own[turn] + core_in[turn].astype(F32)).astype(BF16)
        z_copy(turn).start()

    for turn in range(Z):
        product(turn)
        if turn >= LAG:
            pass_on(turn - LAG)
    for turn in range(Z - LAG, Z - 1):
        pass_on(turn)
    core_copy(Z - 1).wait_recv()
    mine = own[Z - 1] + core_in[Z - 1].astype(F32)
    for turn in range(Z - 2, -1, -1):
        z_copy(turn).wait_recv()
        mine = mine + z_in[turn].astype(F32)
    out[...] = mine.astype(BF16)

    for piece in range(3):
        pair_copy(piece, odd).wait_send()
    for m in (1, 2, 3):
        row_copy(m, pair).wait_send()
    for copy in x_copies:
        copy.wait_send()
    for turn in range(Z):
        core_copy(turn).wait_send()
        if turn < Z - 1:
            z_copy(turn).wait_send()


def on_device(tokens, qkv_weight, beta_logit, log_decay, out_grad):
    dma = pltpu.SemaphoreType.DMA
    return pl.pallas_call(
        kernel,
        out_shape=jax.ShapeDtypeStruct((C, DK), BF16),
        in_specs=[pl.BlockSpec(memory_space=pl.ANY)] * 5,
        out_specs=pl.BlockSpec(memory_space=pltpu.VMEM),
        scratch_shapes=[
            pltpu.VMEM((C, K_PARTS * K_PART), BF16),
            pltpu.VMEM((3, K_PARTS * K_PART, DK), BF16),
            pltpu.VMEM((1, C), F32),
            pltpu.VMEM((1, C), F32),
            pltpu.VMEM((C, DK), BF16),
            pltpu.VMEM((2, ROWS, DK), BF16),
            pltpu.VMEM((4, ROWS, DK), BF16),
            pltpu.VMEM((X, ROWS, DK), BF16),
            pltpu.VMEM((Z, C, DK), BF16),
            pltpu.VMEM((Z, C, DK), BF16),
            pltpu.VMEM((Z, C, DK), F32),
            pltpu.VMEM((Z - 1, C, DK), BF16),
            pltpu.VMEM((Z - 1, C, DK), BF16),
            dma((3 + K_PARTS,)), dma((K_PARTS, 3)),
            dma((3,)), dma((3,)), dma((4,)), dma((4,)), dma((X,)), dma((X,)),
            dma((Z,)), dma((Z,)), dma((Z - 1,)), dma((Z - 1,)),
        ],
        compiler_params=pltpu.CompilerParams(
            collective_id=0, has_side_effects=True, vmem_limit_bytes=63 * 2**20
        ),
        name="delta_rule",
    )(tokens, qkv_weight, beta_logit, log_decay, out_grad)


def solution(mesh):
    return jax.shard_map(
        on_device,
        mesh=mesh,
        in_specs=(
            P("seq", None),
            P(None, None, "head"),
            P("head", "seq"),
            P("head", "seq"),
            P("seq", "head"),
        ),
        out_specs=P("seq", "head"),
        check_vma=False,
    )
```

time: 55.8 us -> 56.7 us (1.016)
  the two profiles are of different devices: /device:TPU:64 before, /device:TPU:1 now
where the time goes in v3:
time: 56.7 us; the launch traced here: 56.5 us
  Pallas kernels  55 us (97%)
  local copies, waits for them, and re-layouts  1.47 us (3%)
    pallas_call x1, Pallas kernels, on_device(): pl.pallas_call(kernel, out_shape=jax.ShapeDtypeStruct((C, DK), BF16), in_...  55 us
    unnamed x1, local copies, waits for them, and re-layouts  1.47 us

profile of v3, /device:TPU:1, one launch (start us, length us, event | category | flops | bytes accessed | tf_op | source)
XLA Modules:
  0.0 56.5 jit_solution(634004079780862176)
XLA Ops:
  0.0 55.0 %delta_rule.1 = bf16[256,128]{1,0:T(8,128)(2,1)} custom-call(bf16[256,2048]{1,0:T(8,128)(2,1)} %tok_hbm.1, bf16[3,2048,128]{2,1,0:T(8,128)(2,1)} %wgt_hbm.1, f32[1,256]{1,0:T(1,128)} %bl_hbm.1, f32[1,256]{1,0:T(1,128)} %ld_hbm.1, bf16[256,128]{1,0:T(8,128)(2,1)} %og_hbm.1), custom_call_target="tpu_custom_call" | custom-call | tf_op jit(solution)/shard_map/delta_rule/pallas_call | solution.py:349
  55.0 1.5 %copy.7 = bf16[256,128]{1,0:T(8,128)(2,1)} copy(bf16[256,128]{1,0:T(8,128)(2,1)} %delta_rule.1) | data formatting | bytes 131072

commit v4 on v3

--- a/solution.py
+++ b/solution.py
@@ -15,7 +15,9 @@
 B_AT, R_AT, A_AT, Z_AT, ROWS = 0, 128, 256, 272, 400
 PIECES = ((R_AT, 144), (B_AT, 128), (Z_AT, 128))
 K_PARTS, K_PART = 2, 1024
-ORDER = (4, -3, 3, -2, 2, -1, 1, 0)
+ORDER = (4, 3, -3, 1, -1, 2, -2, 0)
+HOPS = ((0, 0, 128, 2), (0, 128, 128, -2), (1, 0, 256, 1), (2, 0, 256, -1),
+        (3, 0, 256, 1), (4, 0, 256, -1), (5, 0, 256, 2), (6, 0, 256, -2))
 LAG = 3
 
 
@@ -89,7 +91,7 @@
     pair, odd = y // 2, y % 2
     way = 2 * odd - 1
     peers = [at(dy=m * way) for m in (-2, -1, 1, 2, 3)]
-    peers += [at(dx=m) for m in (1, 2, 3)] + [at(dc=1)] + [at(dz=m) for m in range(1, Z)]
+    peers += [at(dx=m) for m in (1, 2, 3)] + [at(dc=1)] + [at(dz=m) for m in (-2, -1, 1, 2)]
     barrier = pltpu.get_barrier_semaphore()
     for peer in peers:
         pl.semaphore_signal(barrier, inc=1, device_id=peer, device_id_type=MESH)
@@ -291,7 +293,7 @@
     dk = fading * dot(wb, g_out, 1, 1) + dot(et, qb) - dot(h, kb) - opening * dot(yb, s_hi, 1, 1)
     dq = q_inv * (dq - qn * jnp.sum(qn * dq, axis=1, keepdims=True))
     dk = k_inv * (dk - kn * jnp.sum(kn * dk, axis=1, keepdims=True))
-    grads_hi, grads_lo = split(jnp.concatenate([dq, dk, yy], axis=1))
+    grads = jnp.concatenate([dq, dk, yy], axis=1).astype(BF16)
 
     def core_copy(turn):
         return pltpu.make_async_remote_copy(
@@ -299,16 +301,18 @@
             recv_sem=c_r.at[turn], device_id=at(dc=1), device_id_type=MESH,
         )
 
-    def z_copy(turn):
+    def z_copy(hop):
+        turn, start, size, to = HOPS[hop]
+        part = pl.ds(start, size)
         return pltpu.make_async_remote_copy(
-            src_ref=z_out.at[turn], dst_ref=z_in.at[turn], send_sem=z_s.at[turn],
-            recv_sem=z_r.at[turn], device_id=at(dz=ORDER[turn]), device_id_type=MESH,
+            src_ref=z_out.at[turn, part], dst_ref=z_in.at[turn, part], send_sem=z_s.at[hop],
+            recv_sem=z_r.at[hop], device_id=at(dz=to), device_id_type=MESH,
         )
 
     def product(turn):
         to = pl.multiple_of(((z + ORDER[turn] + Z) % Z) * 2 * DK, 2 * DK)
         weight = weights(pl.ds(to, 2 * DK))
-        both = dot(grads_hi, weight, 1, 1) + dot(grads_lo, weight, 1, 1)
+        both = dot(grads, weight, 1, 1)
         left, right = both[:, :DK], both[:, DK:]
         core_out[turn] = jnp.where(core == 0, right, left).astype(BF16)
         core_copy(turn).start()
@@ -316,8 +320,20 @@
 
     def pass_on(turn):
         core_copy(turn).wait_recv()
-        z_out[turn] = (own[turn] + core_in[turn].astype(F32)).astype(BF16)
-        z_copy(turn).start()
+        mine = own[turn] + core_in[turn].astype(F32)
+        if turn == 5:
+            z_copy(0).wait_recv()
+            z_copy(2).wait_recv()
+            far = jnp.concatenate([z_in[0, :128, :].astype(F32), jnp.zeros((128, DK), F32)], axis=0)
+            mine = mine + far + z_in[1].astype(F32)
+        elif turn == 6:
+            z_copy(1).wait_recv()
+            z_copy(3).wait_recv()
+            far = jnp.concatenate([jnp.zeros((128, DK), F32), z_in[0, 128:, :].astype(F32)], axis=0)
+            mine = mine + far + z_in[2].astype(F32)
+        z_out[turn] = mine.astype(BF16)
+        for hop in (0, 1) if turn == 0 else (turn + 1,):
+            z_copy(hop).start()
 
     for turn in range(Z):
         product(turn)
@@ -327,8 +343,8 @@
         pass_on(turn)
     core_copy(Z - 1).wait_recv()
     mine = own[Z - 1] + core_in[Z - 1].astype(F32)
-    for turn in range(Z - 2, -1, -1):
-        z_copy(turn).wait_recv()
+    for turn in range(3, Z - 1):
+        z_copy(turn + 1).wait_recv()
         mine = mine + z_in[turn].astype(F32)
     out[...] = mine.astype(BF16)
 
@@ -340,8 +356,7 @@
         copy.wait_send()
     for turn in range(Z):
         core_copy(turn).wait_send()
-        if turn < Z - 1:
-            z_copy(turn).wait_send()
+        z_copy(turn).wait_send()
 
 
 def on_device(tokens, qkv_weight, beta_logit, log_decay, out_grad):
@@ -367,7 +382,7 @@
             pltpu.VMEM((Z - 1, C, DK), BF16),
             dma((3 + K_PARTS,)), dma((K_PARTS, 3)),
             dma((3,)), dma((3,)), dma((4,)), dma((4,)), dma((X,)), dma((X,)),
-            dma((Z,)), dma((Z,)), dma((Z - 1,)), dma((Z - 1,)),
+            dma((Z,)), dma((Z,)), dma((Z,)), dma((Z,)),
         ],
         compiler_params=pltpu.CompilerParams(
             collective_id=0, has_side_effects=True, vmem_limit_bytes=63 * 2**20

time: 56.7 us -> 51.7 us (0.912)
  Pallas kernels: 55 us -> 50.1 us
    pallas_call x1, Pallas kernels: 55 us -> 50.1 us  [on_device(): pl.pallas_call(kernel, out_shape=jax.ShapeDtypeStruct((C, DK), BF16), in_...]
where the time goes in v4:
time: 51.7 us; the launch traced here: 51.6 us
  Pallas kernels  50.1 us (97%)
  local copies, waits for them, and re-layouts  1.47 us (3%)
    pallas_call x1, Pallas kernels, on_device(): pl.pallas_call(kernel, out_shape=jax.ShapeDtypeStruct((C, DK), BF16), in_...  50.1 us
    unnamed x1, local copies, waits for them, and re-layouts  1.47 us

profile of v4, /device:TPU:1, one launch (start us, length us, event | category | flops | bytes accessed | tf_op | source)
XLA Modules:
  0.0 51.6 jit_solution(9736542679646645717)
XLA Ops:
  0.0 50.1 %delta_rule.1 = bf16[256,128]{1,0:T(8,128)(2,1)} custom-call(bf16[256,2048]{1,0:T(8,128)(2,1)} %tok_hbm.1, bf16[3,2048,128]{2,1,0:T(8,128)(2,1)} %wgt_hbm.1, f32[1,256]{1,0:T(1,128)} %bl_hbm.1, f32[1,256]{1,0:T(1,128)} %ld_hbm.1, bf16[256,128]{1,0:T(8,128)(2,1)} %og_hbm.1), custom_call_target="tpu_custom_call" | custom-call | tf_op jit(solution)/shard_map/delta_rule/pallas_call | solution.py:364
  50.1 1.5 %copy.7 = bf16[256,128]{1,0:T(8,128)(2,1)} copy(bf16[256,128]{1,0:T(8,128)(2,1)} %delta_rule.1) | data formatting | bytes 131072

commit v5 on v4

--- a/solution.py
+++ b/solution.py
@@ -16,8 +16,14 @@
 PIECES = ((R_AT, 144), (B_AT, 128), (Z_AT, 128))
 K_PARTS, K_PART = 2, 1024
 ORDER = (4, 3, -3, 1, -1, 2, -2, 0)
-HOPS = ((0, 0, 128, 2), (0, 128, 128, -2), (1, 0, 256, 1), (2, 0, 256, -1),
-        (3, 0, 256, 1), (4, 0, 256, -1), (5, 0, 256, 2), (6, 0, 256, -2))
+HOPS = (
+    (0, 0, 128, 2), (0, 128, 128, -2),
+    (1, 0, 128, 1), (1, 128, 128, 1), (2, 0, 128, -1), (2, 128, 128, -1),
+    (3, 0, 256, 1), (4, 0, 256, -1),
+    (5, 0, 128, 2), (5, 128, 128, 2), (6, 0, 128, -2), (6, 128, 128, -2),
+)
+SENDS = ((0, 1), (3, 2), (4, 5), (6,), (7,))
+ADDS = ((9, (3,)), (10, (4,)), (8, (0, 2)), (11, (1, 5)))
 LAG = 3
 
 
@@ -320,32 +326,32 @@
 
     def pass_on(turn):
         core_copy(turn).wait_recv()
-        mine = own[turn] + core_in[turn].astype(F32)
-        if turn == 5:
-            z_copy(0).wait_recv()
-            z_copy(2).wait_recv()
-            far = jnp.concatenate([z_in[0, :128, :].astype(F32), jnp.zeros((128, DK), F32)], axis=0)
-            mine = mine + far + z_in[1].astype(F32)
-        elif turn == 6:
-            z_copy(1).wait_recv()
-            z_copy(3).wait_recv()
-            far = jnp.concatenate([jnp.zeros((128, DK), F32), z_in[0, 128:, :].astype(F32)], axis=0)
-            mine = mine + far + z_in[2].astype(F32)
-        z_out[turn] = mine.astype(BF16)
-        for hop in (0, 1) if turn == 0 else (turn + 1,):
+        z_out[turn] = (own[turn] + core_in[turn].astype(F32)).astype(BF16)
+        for hop in SENDS[turn]:
             z_copy(hop).start()
 
     for turn in range(Z):
         product(turn)
-        if turn >= LAG:
+        if LAG <= turn < LAG + 5:
             pass_on(turn - LAG)
-    for turn in range(Z - LAG, Z - 1):
-        pass_on(turn)
+    core_copy(5).wait_recv()
+    core_copy(6).wait_recv()
+    for hop, joins in ADDS:
+        turn, start, size, _ = HOPS[hop]
+        part = pl.ds(start, size)
+        mine = own[turn, part, :] + core_in[turn, part, :].astype(F32)
+        for other in joins:
+            z_copy(other).wait_recv()
+            mine = mine + z_in[HOPS[other][0], part, :].astype(F32)
+        z_out[turn, part, :] = mine.astype(BF16)
+        z_copy(hop).start()
     core_copy(Z - 1).wait_recv()
-    mine = own[Z - 1] + core_in[Z - 1].astype(F32)
-    for turn in range(3, Z - 1):
-        z_copy(turn + 1).wait_recv()
-        mine = mine + z_in[turn].astype(F32)
+    z_copy(6).wait_recv()
+    z_copy(7).wait_recv()
+    mine = own[Z - 1] + core_in[Z - 1].astype(F32) + z_in[3].astype(F32) + z_in[4].astype(F32)
+    for hop in (9, 10, 8, 11):
+        z_copy(hop).wait_recv()
+    mine = mine + z_in[5].astype(F32) + z_in[6].astype(F32)
     out[...] = mine.astype(BF16)
 
     for piece in range(3):
@@ -356,7 +362,8 @@
         copy.wait_send()
     for turn in range(Z):
         core_copy(turn).wait_send()
-        z_copy(turn).wait_send()
+    for hop in range(len(HOPS)):
+        z_copy(hop).wait_send()
 
 
 def on_device(tokens, qkv_weight, beta_logit, log_decay, out_grad):
@@ -382,7 +389,7 @@
             pltpu.VMEM((Z - 1, C, DK), BF16),
             dma((3 + K_PARTS,)), dma((K_PARTS, 3)),
             dma((3,)), dma((3,)), dma((4,)), dma((4,)), dma((X,)), dma((X,)),
-            dma((Z,)), dma((Z,)), dma((Z,)), dma((Z,)),
+            dma((Z,)), dma((Z,)), dma((len(HOPS),)), dma((len(HOPS),)),
         ],
         compiler_params=pltpu.CompilerParams(
             collective_id=0, has_side_effects=True, vmem_limit_bytes=63 * 2**20

time: 51.7 us -> 51 us (0.986)
  Pallas kernels: 50.1 us -> 49.4 us
    pallas_call x1, Pallas kernels: 50.1 us -> 49.4 us  [on_device(): pl.pallas_call(kernel, out_shape=jax.ShapeDtypeStruct((C, DK), BF16), in_...]
where the time goes in v5:
time: 51 us; the launch traced here: 50.9 us
  Pallas kernels  49.4 us (97%)
  local copies, waits for them, and re-layouts  1.47 us (3%)
    pallas_call x1, Pallas kernels, on_device(): pl.pallas_call(kernel, out_shape=jax.ShapeDtypeStruct((C, DK), BF16), in_...  49.4 us
    unnamed x1, local copies, waits for them, and re-layouts  1.47 us

profile of v5, /device:TPU:1, one launch (start us, length us, event | category | flops | bytes accessed | tf_op | source)
XLA Modules:
  0.0 50.9 jit_solution(14630046623774675629)
XLA Ops:
  0.0 49.4 %delta_rule.1 = bf16[256,128]{1,0:T(8,128)(2,1)} custom-call(bf16[256,2048]{1,0:T(8,128)(2,1)} %tok_hbm.1, bf16[3,2048,128]{2,1,0:T(8,128)(2,1)} %wgt_hbm.1, f32[1,256]{1,0:T(1,128)} %bl_hbm.1, f32[1,256]{1,0:T(1,128)} %ld_hbm.1, bf16[256,128]{1,0:T(8,128)(2,1)} %og_hbm.1), custom_call_target="tpu_custom_call" | custom-call | tf_op jit(solution)/shard_map/delta_rule/pallas_call | solution.py:371
  49.4 1.5 %copy.7 = bf16[256,128]{1,0:T(8,128)(2,1)} copy(bf16[256,128]{1,0:T(8,128)(2,1)} %delta_rule.1) | data formatting | bytes 131072

commit v6 on v5

--- a/solution.py
+++ b/solution.py
@@ -96,7 +96,7 @@
         copy.start()
     pair, odd = y // 2, y % 2
     way = 2 * odd - 1
-    peers = [at(dy=m * way) for m in (-2, -1, 1, 2, 3)]
+    peers = [at(dy=m * way) for m in (-2, -1, 1, 2)]
     peers += [at(dx=m) for m in (1, 2, 3)] + [at(dc=1)] + [at(dz=m) for m in (-2, -1, 1, 2)]
     barrier = pltpu.get_barrier_semaphore()
     for peer in peers:
@@ -221,17 +221,25 @@
 
     put(qg.at[pair], a_pair, r_pair, b_pair, z_pair)
 
-    def row_copy(m, slot):
-        part = qg.at[slot]
+    def row_copy(m, piece, slot):
+        start, size = PIECES[piece]
+        part = qg.at[slot, pl.ds(start, size)]
         return pltpu.make_async_remote_copy(
-            src_ref=part, dst_ref=part, send_sem=q_s.at[m], recv_sem=q_r.at[m],
-            device_id=at(dy=m * way), device_id_type=MESH,
-        )
-
-    for m in (3, 2, 1):
-        row_copy(m, pair).start()
-    for m, shift in ((1, way), (2, -way), (3, 2)):
-        row_copy(m, (pair + shift + 4) % 4).wait_recv()
+            src_ref=part, dst_ref=part, send_sem=q_s.at[m - 1, piece], recv_sem=q_r.at[m - 1, piece],
+            device_id=at(dy=(2 if m == 2 else 1) * way), device_id_type=MESH,
+        )
+
+    for m in (2, 1):
+        for piece in range(3):
+            row_copy(m, piece, pair).start()
+    behind_us = (pair - way + 4) % 4
+    for piece in range(3):
+        row_copy(2, piece, behind_us).wait_recv()
+        row_copy(3, piece, behind_us).start()
+    for piece in range(3):
+        row_copy(1, piece, (pair + way + 4) % 4).wait_recv()
+    for piece in range(3):
+        row_copy(3, piece, (pair + 2) % 4).wait_recv()
     pairs = [leaf(qg.at[j]) for j in range(4)]
     quads = [compose(pairs[0], pairs[1]), compose(pairs[2], pairs[3])]
     a_row, r_row, b_row = ahead(quads[0], quads[1])
@@ -356,8 +364,9 @@
 
     for piece in range(3):
         pair_copy(piece, odd).wait_send()
-    for m in (1, 2, 3):
-        row_copy(m, pair).wait_send()
+    for piece in range(3):
+        for m in (1, 2, 3):
+            row_copy(m, piece, behind_us if m == 3 else pair).wait_send()
     for copy in x_copies:
         copy.wait_send()
     for turn in range(Z):
@@ -388,7 +397,7 @@
             pltpu.VMEM((Z - 1, C, DK), BF16),
             pltpu.VMEM((Z - 1, C, DK), BF16),
             dma((3 + K_PARTS,)), dma((K_PARTS, 3)),
-            dma((3,)), dma((3,)), dma((4,)), dma((4,)), dma((X,)), dma((X,)),
+            dma((3,)), dma((3,)), dma((3, 3)), dma((3, 3)), dma((X,)), dma((X,)),
             dma((Z,)), dma((Z,)), dma((len(HOPS),)), dma((len(HOPS),)),
         ],
         compiler_params=pltpu.CompilerParams(

time: 51 us -> 50.2 us (0.984)
  Pallas kernels: 49.4 us -> 48.5 us
    pallas_call x1, Pallas kernels: 49.4 us -> 48.5 us  [on_device(): pl.pallas_call(kernel, out_shape=jax.ShapeDtypeStruct((C, DK), BF16), in_...]
where the time goes in v6:
time: 50.2 us; the launch traced here: 50 us
  Pallas kernels  48.5 us (97%)
  local copies, waits for them, and re-layouts  1.47 us (3%)
    pallas_call x1, Pallas kernels, on_device(): pl.pallas_call(kernel, out_shape=jax.ShapeDtypeStruct((C, DK), BF16), in_...  48.5 us
    unnamed x1, local copies, waits for them, and re-layouts  1.47 us

profile of v6, /device:TPU:1, one launch (start us, length us, event | category | flops | bytes accessed | tf_op | source)
XLA Modules:
  0.0 50.0 jit_solution(6423267636570270464)
XLA Ops:
  0.0 48.5 %delta_rule.1 = bf16[256,128]{1,0:T(8,128)(2,1)} custom-call(bf16[256,2048]{1,0:T(8,128)(2,1)} %tok_hbm.1, bf16[3,2048,128]{2,1,0:T(8,128)(2,1)} %wgt_hbm.1, f32[1,256]{1,0:T(1,128)} %bl_hbm.1, f32[1,256]{1,0:T(1,128)} %ld_hbm.1, bf16[256,128]{1,0:T(8,128)(2,1)} %og_hbm.1), custom_call_target="tpu_custom_call" | custom-call | tf_op jit(solution)/shard_map/delta_rule/pallas_call | solution.py:380
  48.5 1.5 %copy.7 = bf16[256,128]{1,0:T(8,128)(2,1)} copy(bf16[256,128]{1,0:T(8,128)(2,1)} %delta_rule.1) | data formatting | bytes 131072

commit v7 on v6

--- a/solution.py
+++ b/solution.py
@@ -213,14 +213,6 @@
     def pick(flag, one, other):
         return tuple(jnp.where(flag, p, o) for p, o in zip(one, other))
 
-    for piece in range(3):
-        pair_copy(piece, 1 - odd).wait_recv()
-    early, late = leaf(ag.at[0]), leaf(ag.at[1])
-    a_pair, r_pair, b_pair = ahead(early, late)
-    _, _, z_pair = behind(early, late)
-
-    put(qg.at[pair], a_pair, r_pair, b_pair, z_pair)
-
     def row_copy(m, piece, slot):
         start, size = PIECES[piece]
         part = qg.at[slot, pl.ds(start, size)]
@@ -229,9 +221,27 @@
             device_id=at(dy=(2 if m == 2 else 1) * way), device_id_type=MESH,
         )
 
-    for m in (2, 1):
-        for piece in range(3):
+    def send_pair(piece):
+        for m in (2, 1):
             row_copy(m, piece, pair).start()
+
+    pair_copy(0, 1 - odd).wait_recv()
+    a_0, a_1 = scale_of(ag.at[0]), scale_of(ag.at[1])
+    r_0, r_1 = ag[0, pl.ds(R_AT, DK), :], ag[1, pl.ds(R_AT, DK), :]
+    r_pair = a_1 * r_0.astype(F32) + a_0 * r_1.astype(F32) + dot(r_1, r_0)
+    put_r(qg.at[pair], a_0 * a_1, r_pair)
+    send_pair(0)
+    pair_copy(1, 1 - odd).wait_recv()
+    b_0 = ag[0, pl.ds(B_AT, DK), :]
+    b_pair = a_1 * b_0.astype(F32) + ag[1, pl.ds(B_AT, DK), :].astype(F32) + dot(r_1, b_0)
+    qg[pair, pl.ds(B_AT, DK), :] = b_pair.astype(BF16)
+    send_pair(1)
+    pair_copy(2, 1 - odd).wait_recv()
+    z_1 = ag[1, pl.ds(Z_AT, DK), :]
+    z_pair = a_0 * z_1.astype(F32) + ag[0, pl.ds(Z_AT, DK), :].astype(F32) + dot(r_0, z_1, 0, 0)
+    qg[pair, pl.ds(Z_AT, DK), :] = z_pair.astype(BF16)
+    send_pair(2)
+    early, late = leaf(ag.at[0]), leaf(ag.at[1])
     behind_us = (pair - way + 4) % 4
     for piece in range(3):
         row_copy(2, piece, behind_us).wait_recv()

time: 50.2 us -> 50.2 us (level)
  no operation moved by 1% of the time
where the time goes in v7:
time: 50.2 us; the launch traced here: 50.1 us
  Pallas kernels  48.6 us (97%)
  local copies, waits for them, and re-layouts  1.47 us (3%)
    pallas_call x1, Pallas kernels, on_device(): pl.pallas_call(kernel, out_shape=jax.ShapeDtypeStruct((C, DK), BF16), in_...  48.6 us
    unnamed x1, local copies, waits for them, and re-layouts  1.47 us

profile of v7, /device:TPU:1, one launch (start us, length us, event | category | flops | bytes accessed | tf_op | source)
XLA Modules:
  0.0 50.1 jit_solution(7886987473713313711)
XLA Ops:
  0.0 48.6 %delta_rule.1 = bf16[256,128]{1,0:T(8,128)(2,1)} custom-call(bf16[256,2048]{1,0:T(8,128)(2,1)} %tok_hbm.1, bf16[3,2048,128]{2,1,0:T(8,128)(2,1)} %wgt_hbm.1, f32[1,256]{1,0:T(1,128)} %bl_hbm.1, f32[1,256]{1,0:T(1,128)} %ld_hbm.1, bf16[256,128]{1,0:T(8,128)(2,1)} %og_hbm.1), custom_call_target="tpu_custom_call" | custom-call | tf_op jit(solution)/shard_map/delta_rule/pallas_call | solution.py:390
  48.6 1.5 %copy.7 = bf16[256,128]{1,0:T(8,128)(2,1)} copy(bf16[256,128]{1,0:T(8,128)(2,1)} %delta_rule.1) | data formatting | bytes 131072
